TPU v7x, 128 devices: a whole 4x4x4 slice. The times are simulated.
128 devices in a mesh: dp: 8 (over y_hi, x), mp: 16 (over y_lo, z, core).
Axes of the slice: x: 4, y: 4 (y_hi: 2, y_lo: 2; y = y_hi * 2 + y_lo), z: 4, core: 2. Of those that a mesh axis runs over, the one named last changes fastest.
Arguments:
- tokens: bfloat16 [4096, 4096], P('dp', 'mp'), may hold values from -6 to 6
- cotangent: bfloat16 [4096, 4096], P('dp', 'mp'), may hold values from -6 to 6
- w_in: bfloat16 [2, 4096, 10240], P(None, None, 'mp'), may hold values from -0.09375 to 0.09375
- w_out: bfloat16 [10240, 4096], P('mp'), may hold values from -0.0625 to 0.0625
- row_in: float32 [2, 4096], P(None, 'dp'), may hold values from 0.01 to 2
- col_in: float32 [2, 10240], P(None, 'mp'), may hold values from 0.01 to 2
- row_out: float32 [10240], P('mp'), may hold values from 0.01 to 2
- col_out: float32 [4096], P('dp'), may hold values from 0.01 to 2
Outputs:
- input_grad: bfloat16 [4096, 4096], P('dp', 'mp')
- update_in: bfloat16 [2, 4096, 10240], P(None, 'dp', 'mp')
- update_out: bfloat16 [10240, 4096], P('mp', 'dp')
- row_in_new: float32 [2, 4096], P(None, 'dp')
- col_in_new: float32 [2, 10240], P(None, 'mp')
- row_out_new: float32 [10240], P('mp')
- col_out_new: float32 [4096], P('dp')
All inputs are finite; a program needn't handle non-finite values.
Results may differ from a plain program's by a relative error of at most 0.025.
Values may be sent and summed in bfloat16 or wider, within the bound.
A program may use at most 128 MiB of HBM per device.

v0:
```python
import math

import jax
import jax.numpy as jnp
from jax import lax
from jax.sharding import PartitionSpec as P


def gelu_pair(values):
    root = math.sqrt(2.0 / math.pi)
    tanh_val = jnp.tanh(root * (values + 0.044715 * values * values * values))
    activated = 0.5 * values * (1.0 + tanh_val)
    slopes = 0.5 * (1.0 + tanh_val) + 0.5 * values * (1.0 - tanh_val * tanh_val) * root * (
        1.0 + 3.0 * 0.044715 * values * values
    )
    return (activated, slopes)


def contract(left, right, left_dim, right_dim):
    return lax.dot_general(
        left, right, (((left_dim,), (right_dim,)), ((), ())), preferred_element_type=jnp.float32
    )


def local(tokens, cotangent, w_in, w_out, row_in, col_in, row_out, col_out):
    tok_full, cot_full = (
        lax.all_gather(tokens, "mp", axis=1, tiled=True),
        lax.all_gather(cotangent, "mp", axis=1, tiled=True),
    )
    gate_pre = jnp.dot(tok_full, w_in[0], preferred_element_type=jnp.float32)
    up_pre = jnp.dot(tok_full, w_in[1], preferred_element_type=jnp.float32)
    activated, slopes = gelu_pair(gate_pre)
    hidden = (activated * up_pre).astype(jnp.bfloat16)
    d_hidden = contract(cot_full, w_out, 1, 1)
    d_gate = (d_hidden * up_pre * slopes).astype(jnp.bfloat16)
    d_up = (d_hidden * activated).astype(jnp.bfloat16)
    input_terms = contract(d_gate, w_in[0], 1, 1) + contract(d_up, w_in[1], 1, 1)
    input_grad = lax.psum_scatter(
        input_terms.astype(jnp.bfloat16), "mp", scatter_dimension=1, tiled=True
    )
    factor = 1.0 / math.sqrt(tokens.shape[0] * lax.axis_size("dp"))
    first = contract(tok_full, d_gate, 0, 0)
    second = contract(tok_full, d_up, 0, 0)
    third = contract(cot_full, hidden, 0, 0)
    gradients = lax.psum_scatter(
        (jnp.stack([first, second, third], axis=1) * factor).astype(jnp.bfloat16),
        "dp",
        scatter_dimension=0,
        tiled=True,
    ).astype(jnp.float32)
    grad_in = jnp.moveaxis(gradients[:, :2, :], 1, 0)
    grad_out_t = gradients[:, 2, :]
    nu_in = jnp.minimum(row_in[:, :, None], col_in[:, None, :]) + grad_in * grad_in
    nu_out_t = jnp.minimum(col_out[:, None], row_out[None, :]) + grad_out_t * grad_out_t
    row_local = jnp.concatenate(
        [jnp.max(nu_in, axis=2), jnp.max(nu_out_t, axis=1)[None, :]], axis=0
    )
    col_local = jnp.concatenate(
        [jnp.max(nu_in, axis=1), jnp.max(nu_out_t, axis=0)[None, :]], axis=0
    )
    row_max = lax.pmax(row_local, "mp")
    col_max = lax.pmax(col_local, "dp")
    row_in_new = row_max[:2]
    col_out_new = row_max[2]
    col_in_new = col_max[:2]
    row_out_new = col_max[2]
    update_in = (grad_in / jnp.sqrt(nu_in)).astype(jnp.bfloat16)
    update_out = (grad_out_t / jnp.sqrt(nu_out_t)).T.astype(jnp.bfloat16)
    return (input_grad, update_in, update_out, row_in_new, col_in_new, row_out_new, col_out_new)


def solution(mesh):
    return jax.shard_map(
        local,
        mesh=mesh,
        in_specs=(
            P("dp", "mp"),
            P("dp", "mp"),
            P(None, None, "mp"),
            P("mp", None),
            P(None, "dp"),
            P(None, "mp"),
            P("mp"),
            P("dp"),
        ),
        out_specs=(
            P("dp", "mp"),
            P(None, "dp", "mp"),
            P("mp", "dp"),
            P(None, "dp"),
            P(None, "mp"),
            P("mp"),
            P("dp"),
        ),
        check_vma=False,
    )
```

profile of v0, /device:TPU:0, one launch (start us, length us, event | category | flops | bytes accessed | tf_op | source)
XLA Modules:
  0.0 397.5 jit_solution(2185627648738535958)
XLA Ops:
  7.2 0.0 all-gather.5.cloned.1.call-start
  7.2 0.7 all-gather.5.cloned.1.call-update
  7.9 0.0 all-gather.3.cloned.1.call-start
  7.9 0.7 all-gather.3.cloned.1.call-update
  8.6 0.0 reduce-scatter.5.cloned.1.call-start
  8.7 48.9 %all-gather.5.cloned.1.call-done = bf16[512,4096]{1,0:T(8,128)(2,1)} async-done(((bf16[512,256]{1,0:T(8,128)(2,1)}), bf16[512,4096]{1,0:T(8,128)(2,1)}) %all-gather.5.cloned.1.call-update) | async-done | bytes 4194320 | tf_op jit(solution)/shard_map/all_gather | solution.py:27
  57.6 6.9 %fusion.3 = f32[512,640]{1,0:T(8,128)S(1)} fusion(bf16[512,4096]{1,0:T(8,128)(2,1)} %all-gather.5.cloned.1.call-done, bf16[2,4096,640]{2,1,0:T(8,128)(2,1)} %param.10), kind=kOutput, calls=%fused_computation.8 | convolution fusion | flops 2684354560 | bytes 10747904 | tf_op jit(solution)/shard_map/dot_general | solution.py:30
  64.5 5.9 %fusion.6 = f32[512,640]{1,0:T(8,128)S(1)} fusion(bf16[512,4096]{1,0:T(8,128)(2,1)S(1)} %copy-done, bf16[2,4096,640]{2,1,0:T(8,128)(2,1)} %param.10), kind=kOutput, calls=%fused_computation.11 | convolution fusion | flops 2684354560 | bytes 10747904 | tf_op jit(solution)/shard_map/dot_general | solution.py:31
  70.4 34.3 %all-gather.3.cloned.1.call-done = bf16[512,4096]{1,0:T(8,128)(2,1)} async-done(((bf16[512,256]{1,0:T(8,128)(2,1)}), bf16[512,4096]{1,0:T(8,128)(2,1)}) %all-gather.3.cloned.1.call-update) | async-done | bytes 4194320 | tf_op jit(solution)/shard_map/all_gather | solution.py:28
  104.7 5.2 %convolution_bitcast_fusion = f32[4096,1,640]{0,2,1:T(8,128)S(1)} fusion(bf16[512,4096]{1,0:T(8,128)(2,1)} %all-gather.3.cloned.1.call-done, f32[512,640]{1,0:T(8,128)S(1)} %fusion.6, f32[512,640]{1,0:T(8,128)S(1)} %fusion.3), kind=kOutput, calls=%fused_computation.3 | convolution fusion | flops 2687631360 | bytes 17301504 | tf_op jit(solution)/shard_map/dot_general | solution.py:20
  110.0 4.1 %multiply_convert_fusion.3 = (bf16[512,640]{1,0:T(8,128)(2,1)S(1)}, bf16[512,640]{1,0:T(8,128)(2,1)S(1)}) fusion(f32[512,640]{1,0:T(8,128)S(1)} %fusion.3, f32[512,640]{1,0:T(8,128)S(1)} %fusion.6, bf16[512,4096]{1,0:T(8,128)(2,1)S(1)} %copy-done.2, bf16[640,4096]{1,0:T(8,128)(2,1)S(1)} %copy-done.9), kind=kOutput, calls=%fused_computation.37 | convolution fusion | flops 2691891200 | bytes 13369344 | tf_op jit(solution)/shard_map/dot_general | solution.py:20
  114.1 0.0 copy-start.3
  114.1 3.0 convolution_bitcast_fusion.1
  117.1 5.7 %convolution_bitcast_fusion.2 = f32[4096,1,640]{0,2,1:T(8,128)} fusion(bf16[512,640]{1,0:T(8,128)(2,1)S(1)} %get-tuple-element.21, bf16[512,4096]{1,0:T(8,128)(2,1)S(1)} %copy-done.1), kind=kOutput, calls=%fused_computation.5 | convolution fusion | flops 2684354560 | bytes 15335424 | tf_op jit(solution)/shard_map/dot_general | solution.py:20
  122.8 11.8 %fusion = bf16[4096,3,640]{0,2,1:T(8,128)(2,1)} fusion(f32[4096,1,640]{0,2,1:T(8,128)S(1)} %convolution_bitcast_fusion, f32[4096,1,640]{0,2,1:T(8,128)S(1)} %convolution_bitcast_fusion.1, f32[4096,1,640]{0,2,1:T(8,128)} %convolution_bitcast_fusion.2), kind=kLoop, calls=%fused_computation.1 | loop fusion | flops 31457280 | bytes 47185920 | tf_op jit(solution)/shard_map/convert_element_type | solution.py:46
  134.6 0.0 reduce-scatter.5.cloned.1.call-update
  134.6 0.0 reduce-scatter.3.cloned.1.call-start
  134.7 1.0 copy-done.4
  135.7 5.4 %fusion.1 = f32[512,4096]{1,0:T(8,128)S(1)} fusion(bf16[512,640]{1,0:T(8,128)(2,1)S(1)} %copy-done.4, bf16[2,4096,640]{2,1,0:T(8,128)(2,1)} %param.10), kind=kOutput, calls=%fused_computation.6 | convolution fusion | flops 2684354560 | bytes 14286848 | tf_op jit(solution)/shard_map/dot_general | solution.py:20
  141.1 7.6 %add_convert_fusion = bf16[512,4096]{1,0:T(8,128)(2,1)} fusion(f32[512,4096]{1,0:T(8,128)S(1)} %fusion.1, bf16[512,640]{1,0:T(8,128)(2,1)S(1)} %get-tuple-element.20, bf16[2,4096,640]{2,1,0:T(8,128)(2,1)} %param.10), kind=kOutput, calls=%fused_computation.2 | convolution fusion | flops 2688548864 | bytes 18481152 | tf_op jit(solution)/shard_map/dot_general | solution.py:20
  148.7 0.0 reduce-scatter.3.cloned.1.call-update
  148.8 165.6 %reduce-scatter.5.cloned.1.call-done = bf16[512,3,640]{0,2,1:T(8,128)(2,1)} async-done(((bf16[4096,3,640]{0,2,1:T(8,128)(2,1)}), bf16[512,3,640]{0,2,1:T(8,128)(2,1)}) %reduce-scatter.5.cloned.1.call-update) | async-done | bytes 1966096 | tf_op jit(solution)/shard_map/reduce_scatter | solution.py:45
  314.4 2.1 convert_element_type.32
  316.5 1.2 fusion.21
  317.7 0.9 fusion.12
  318.7 29.5 %pmax.14 = f32[3,512]{1,0:T(4,128)S(1)} all-reduce(f32[3,512]{1,0:T(4,128)S(1)} %pad_maximum_fusion.1), channel_id=1, replica_groups=mesh['dp'=8,'mp'=16] {'mp'}, use_global_device_ids=true, to_apply=%region_4.0 | all-reduce | flops 1536 | bytes 12288 | tf_op jit(solution)/shard_map/pmax | solution.py:61
  348.2 0.6 slice.39
  348.8 0.6 slice.36
  349.4 38.9 %pmax.15 = f32[3,640]{1,0:T(4,128)S(1)} all-reduce(f32[3,640]{1,0:T(4,128)S(1)} %pad_maximum_fusion), channel_id=1, replica_groups=mesh['dp'=8,'mp'=16] {'dp'}, use_global_device_ids=true, to_apply=%region_7.0 | all-reduce | flops 1920 | bytes 15360 | tf_op jit(solution)/shard_map/pmax | solution.py:62
  388.3 0.6 slice.37
  388.9 1.4 copy.15
  390.4 0.6 slice_reduce_fusion
  (22 shorter events, 0.1 us)
Async XLA Ops:
  7.2 50.5 %all-gather.5.cloned.1.call-start = ((), (), s32[]{:S(2)}) async-start(), calls=%async_computation.3 | async-start | bytes 4456448 | tf_op jit(solution)/shard_map/all_gather | solution.py:27
  7.9 96.8 %all-gather.3.cloned.1.call-start = ((), (), s32[]{:S(2)}) async-start(), calls=%async_computation.2 | async-start | bytes 4456448 | tf_op jit(solution)/shard_map/all_gather | solution.py:28
  8.6 305.7 %reduce-scatter.5.cloned.1.call-start = ((), (), s32[]{:S(2)}) async-start(), calls=%async_computation.5 | async-start | bytes 17694720 | tf_op jit(solution)/shard_map/reduce_scatter | solution.py:45
  57.6 6.9 %copy-start = (bf16[512,4096]{1,0:T(8,128)(2,1)S(1)}, bf16[512,4096]{1,0:T(8,128)(2,1)}, u32[]{:S(2)}) copy-start(bf16[512,4096]{1,0:T(8,128)(2,1)} %all-gather.5.cloned.1.call-done) | copy-start | bytes 12582916
  104.7 5.2 %copy-start.2 = (bf16[512,4096]{1,0:T(8,128)(2,1)S(1)}, bf16[512,4096]{1,0:T(8,128)(2,1)}, u32[]{:S(2)}) copy-start(bf16[512,4096]{1,0:T(8,128)(2,1)} %all-gather.3.cloned.1.call-done) | copy-start | bytes 12582916
  104.7 5.3 %copy-start.9 = (bf16[640,4096]{1,0:T(8,128)(2,1)S(1)}, bf16[640,4096]{1,0:T(8,128)(2,1)}, u32[]{:S(2)}) copy-start(bf16[640,4096]{1,0:T(8,128)(2,1)} %param.11) | copy-start | bytes 15728644
  110.0 4.2 %copy-start.1 = (bf16[512,4096]{1,0:T(8,128)(2,1)S(1)}, bf16[512,4096]{1,0:T(8,128)(2,1)}, u32[]{:S(2)}) copy-start(bf16[512,4096]{1,0:T(8,128)(2,1)} %all-gather.5.cloned.1.call-done) | copy-start | bytes 12582916
  114.1 3.0 copy-start.3
  134.6 1.1 copy-start.4
  134.6 256.3 %reduce-scatter.3.cloned.1.call-start = ((), (), s32[]{:S(2)}) async-start(), calls=%async_computation.4 | async-start | bytes 4456448 | tf_op jit(solution)/shard_map/reduce_scatter | solution.py:38
  148.8 167.7 %copy-start.6 = (f32[640]{0:T(1024)S(1)}, f32[640]{0:T(1024)}, u32[]{:S(2)}) copy-start(f32[640]{0:T(1024)} %param.14) | copy-start | bytes 7684
  148.8 167.7 %copy-start.8 = (f32[512]{0:T(512)S(1)}, f32[512]{0:T(512)}, u32[]{:S(2)}) copy-start(f32[512]{0:T(512)} %param.15) | copy-start | bytes 6148
  148.8 168.9 %copy-start.5 = (f32[2,640]{1,0:T(2,128)S(1)}, f32[2,640]{1,0:T(2,128)}, u32[]{:S(2)}) copy-start(f32[2,640]{1,0:T(2,128)} %param.13) | copy-start | bytes 15364
  148.8 168.9 %copy-start.7 = (f32[2,512]{1,0:T(2,128)S(1)}, f32[2,512]{1,0:T(2,128)}, u32[]{:S(2)}) copy-start(f32[2,512]{1,0:T(2,128)} %param.12) | copy-start | bytes 12292
Sparse Core Ops, SparseCore 0:
  9.6 47.9 all-gather.4
  59.2 45.4 all-gather.2
  134.8 179.5 reduce-scatter.4
  317.3 65.2 reduce-scatter.2
where the time goes:
time: 398 us; the launch traced here: 397 us
  waiting for transfers between devices  250 us (63%)
  blocking collectives  68.4 us (17%)
  matrix products  43.8 us (11%)
  other arithmetic  16.1 us (4%)
  between operations  13.9 us (3%)
  local copies, waits for them, and re-layouts  4.87 us (1%)
    reduce_scatter x1, waiting for transfers between devices, local(): lax.psum_scatter((jnp.stack([first, second, third], axis=1) * factor).ast...  166 us
    all_gather x1, waiting for transfers between devices, local(): lax.all_gather(tokens, 'mp', axis=1, tiled=True)  48.9 us
    pmax x1, blocking collectives, local(): col_max = lax.pmax(col_local, 'dp')  38.9 us
    all_gather x1, waiting for transfers between devices, local(): lax.all_gather(cotangent, 'mp', axis=1, tiled=True)  34.3 us
    dot_general x6, matrix products, contract(): lax.dot_general(left, right, (((left_dim,), (right_dim,)), ((), ())), pre...  31 us
    pmax x1, blocking collectives, local(): row_max = lax.pmax(row_local, 'mp')  29.5 us
    convert_element_type x1, other arithmetic, local(): (jnp.stack([first, second, third], axis=1) * factor).astype(jnp.bfloat16)  11.8 us
  transfers between devices with their start and end apart: 4, of which 3 were waited for; matrix products, arithmetic and copies ran while one was open for 9% of the time, Pallas kernels for 0%

commit v1 on v0

v1 whole, which is shorter than its diff:
```python
import functools
import math

import jax
import jax.numpy as jnp
from jax import lax
from jax.experimental import pallas as pl
from jax.experimental.pallas import tpu as pltpu
from jax.sharding import PartitionSpec as P

BF = jnp.bfloat16
F32 = jnp.float32
MESH = pl.DeviceIdType.MESH
ROOT = math.sqrt(2.0 / math.pi)

HID, DUP, DGATE = 0, 1, 2


def nn(a, b):
    return jnp.dot(a, b, preferred_element_type=F32)


def nt(a, b):
    return lax.dot_general(a, b, (((1,), (1,)), ((), ())), preferred_element_type=F32)


def tn(a, b):
    return lax.dot_general(a, b, (((0,), (0,)), ((), ())), preferred_element_type=F32)


def kernel(
    factor,
    tok_in,
    cot_in,
    w_in,
    w_out,
    row_in,
    col_in,
    row_out,
    col_out,
    ig_o,
    upd_in_o,
    upd_out_o,
    row_in_o,
    col_in_o,
    row_out_o,
    col_out_o,
    full,
    wi,
    wo,
    pre,
    act,
    other,
    accs,
    gsend,
    grecv,
    igs,
    igr,
    igz,
    igy,
    rowv,
    rbuf,
    cbuf,
    lsem,
    ssem,
    rsem,
    xssem,
    xrsem,
):
    dp, mp = lax.axis_index("dp"), lax.axis_index("mp")
    yh, x = dp // 4, dp % 4
    yl, z, c = mp // 8, (mp // 2) % 4, mp % 2
    t_rows, h_cols = pre.shape[1], pre.shape[2]
    half = t_rows // 2

    def dev(dx=0, dyh=0, dyl=0, dz=0, dc=0):
        return (
            lax.rem(yh + dyh, 2) * 4 + lax.rem(x + dx, 4),
            lax.rem(yl + dyl, 2) * 8 + lax.rem(z + dz, 4) * 2 + lax.rem(c + dc, 2),
        )

    def chip(dy, dz):
        return lax.rem(yl + dy, 2) * 4 + lax.rem(z + dz, 4)

    peers = [
        dev(dz=1), dev(dz=3), dev(dz=2), dev(dyl=1), dev(dc=1), dev(dyl=1, dc=1),
        dev(dx=1), dev(dx=3), dev(dx=2), dev(dyh=1),
    ]
    barrier = pltpu.get_barrier_semaphore()
    for peer in peers:
        pl.semaphore_signal(barrier, inc=1, device_id=peer, device_id_type=MESH)

    loads = []

    def load(src, dst):
        copy = pltpu.make_async_copy(src, dst, lsem.at[len(loads)])
        copy.start()
        loads.append(copy)
        return copy

    own_tok = load(tok_in, full.at[0, mp])
    own_cot = load(cot_in, full.at[1, mp])
    load_w = [load(w_in.at[0], wi.at[0]), load(w_in.at[1], wi.at[1])]
    load_wo = load(w_out, wo)

    sent = []

    def send(src, dst, device):
        i = len(sent)
        copy = pltpu.make_async_remote_copy(
            src_ref=src, dst_ref=dst, send_sem=ssem.at[i], recv_sem=rsem.at[i],
            device_id=device, device_id_type=MESH,
        )
        copy.start()
        sent.append(copy)
        return copy

    xsent = [[], []]

    def xsend(t, dy, dz, src=None):
        origin_z = lax.rem(z + dz, 4)
        origin_y = lax.rem(yl + dy, 2)
        dx = lax.rem(origin_z + 4 - x, 4)
        there = jnp.maximum(dx - 1, 0)
        i = len(xsent[t])
        copy = pltpu.make_async_remote_copy(
            src_ref=full.at[t, chip(dy, dz) * 2 + c] if src is None else src,
            dst_ref=other.at[t, there, origin_y, c],
            send_sem=xssem.at[t, i], recv_sem=xrsem.at[t, there, origin_y],
            device_id=(yh * 4 + origin_z, mp), device_id_type=MESH,
        )
        xsent[t].append((dx != 0, copy))

        @pl.when(dx != 0)
        def _():
            copy.start()

    ag = [{}, {}]
    sib = [{}, {}]

    def share(t, dy, dz, src=None):
        slot = full.at[t, chip(dy, dz) * 2 + c]
        sib[t][(dy, dz)] = send(slot if src is None else src, slot, dev(dc=1))
        xsend(t, dy, dz, src)

    def ag_start(t):
        src = tok_in if t == 0 else cot_in
        slot = full.at[t, mp]
        ag[t]["z-"] = send(src, slot, dev(dz=1))
        ag[t]["z+"] = send(src, slot, dev(dz=3))
        ag[t]["y"] = send(src, slot, dev(dyl=1))
        share(t, 0, 0, src)

    def ag_1(t):
        ag[t]["z-"].wait_recv()
        slot = full.at[t, chip(0, 3) * 2 + c]
        ag[t]["zz-"] = send(slot.at[pl.ds(0, half)], slot.at[pl.ds(0, half)], dev(dz=1))
        share(t, 0, 3)
        ag[t]["z+"].wait_recv()
        slot = full.at[t, chip(0, 1) * 2 + c]
        ag[t]["zz+"] = send(slot.at[pl.ds(half, half)], slot.at[pl.ds(half, half)], dev(dz=3))
        share(t, 0, 1)
        ag[t]["y"].wait_recv()
        slot = full.at[t, chip(1, 0) * 2 + c]
        ag[t]["yz-"] = send(slot, slot, dev(dz=1))
        ag[t]["yz+"] = send(slot, slot, dev(dz=3))
        share(t, 1, 0)

    def ag_2a(t):
        slot = full.at[t, chip(0, 2) * 2 + c]
        ag[t]["zz-"].wait_recv()
        ag[t]["yzz-"] = send(slot.at[pl.ds(0, half)], slot.at[pl.ds(0, half)], dev(dyl=1))
        ag[t]["zz+"].wait_recv()
        ag[t]["yzz+"] = send(slot.at[pl.ds(half, half)], slot.at[pl.ds(half, half)], dev(dyl=1))
        share(t, 0, 2)

    def ag_2b(t):
        ag[t]["yz-"].wait_recv()
        share(t, 1, 3)
        ag[t]["yz+"].wait_recv()
        share(t, 1, 1)

    def ag_3(t):
        ag[t]["yzz-"].wait_recv()
        ag[t]["yzz+"].wait_recv()
        share(t, 1, 2)

    def forward(dy, dz, first=False):
        sib[0][(dy, dz)].wait_recv()
        m = chip(dy, dz)

        @pl.loop(0, 4)
        def _(i):
            k, rows = i // 2, pl.ds(pl.multiple_of((i % 2) * half, half), half)
            part = nn(full[0, m * 2, rows], wi[k, pl.ds(pl.multiple_of(m * 512, 512), 256)]) + nn(
                full[0, m * 2 + 1, rows], wi[k, pl.ds(pl.multiple_of(m * 512 + 256, 256), 256)]
            )
            if first:
                pre[k, rows] = part
            else:
                pre[k, rows] += part

    def backward(dy, dz, first=False):
        sib[1][(dy, dz)].wait_recv()
        m = chip(dy, dz)

        @pl.loop(0, 2)
        def _(i):
            rows = pl.ds(pl.multiple_of(i * half, half), half)
            part = nt(full[1, m * 2, rows], wo[:, pl.ds(pl.multiple_of(m * 512, 512), 256)]) + nt(
                full[1, m * 2 + 1, rows], wo[:, pl.ds(pl.multiple_of(m * 512 + 256, 256), 256)]
            )
            if first:
                pre[2, rows] = part
            else:
                pre[2, rows] += part

    step = 32

    def make_hidden():
        @pl.loop(0, t_rows // step)
        def _(i):
            rows = pl.ds(pl.multiple_of(i * step, step), step)
            v = pre[0, rows]
            up = pre[1, rows]
            t = jnp.tanh(ROOT * (v + 0.044715 * v * v * v))
            activated = 0.5 * v * (1.0 + t)
            slopes = 0.5 * (1.0 + t) + 0.5 * v * (1.0 - t * t) * ROOT * (
                1.0 + 3.0 * 0.044715 * v * v
            )
            act[HID, 0, rows] = (activated * up).astype(BF)
            pre[0, rows] = activated
            pre[1, rows] = up * slopes

    def make_d():
        @pl.loop(0, t_rows // step)
        def _(i):
            rows = pl.ds(pl.multiple_of(i * step, step), step)
            d = pre[2, rows]
            act[DUP, 0, rows] = (d * pre[0, rows]).astype(BF)
            act[DGATE, 0, rows] = (d * pre[1, rows]).astype(BF)

    xg = [{}, {}, {}]
    lo, hi = pl.ds(0, half), pl.ds(half, half)

    def xg_start(q):
        own = act.at[q, 0]
        xg[q]["a-"] = send(own.at[lo], act.at[q, 1].at[lo], dev(dx=1))
        xg[q]["b+"] = send(own.at[hi], act.at[q, 3].at[hi], dev(dx=3))
        xg[q]["b-"] = send(own.at[hi], act.at[q, 1].at[hi], dev(dx=1))
        xg[q]["a+"] = send(own.at[lo], act.at[q, 3].at[lo], dev(dx=3))

    def xg_relay(q):
        xg[q]["a-"].wait_recv()
        xg[q]["aa"] = send(act.at[q, 1].at[lo], act.at[q, 2].at[lo], dev(dx=1))
        xg[q]["b+"].wait_recv()
        xg[q]["bb"] = send(act.at[q, 3].at[hi], act.at[q, 2].at[hi], dev(dx=3))

    def xg_rest(q):
        xg[q]["b-"].wait_recv()
        xg[q]["a+"].wait_recv()

    def xg_last(q):
        xg[q]["aa"].wait_recv()
        xg[q]["bb"].wait_recv()

    osib = [{}, {}]

    def other_share(t):
        for r in range(3):
            for h in range(2):
                slot = other.at[t, r, h, c]
                pltpu.make_async_remote_copy(
                    src_ref=slot, dst_ref=slot, send_sem=xssem.at[t, 0], recv_sem=xrsem.at[t, r, h],
                    device_id=dev(dc=1), device_id_type=MESH,
                ).wait_recv()
                osib[t][(r, h)] = send(slot, slot, dev(dc=1))

    def other_wait(t):
        for copy in osib[t].values():
            copy.wait_recv()

    gs = [None] * 3

    def wgrad(q, r, first=False, last=False):
        t = 1 if q == HID else 0

        @pl.loop(0, 4)
        def _(i):
            part_kept, b = i // 2, i % 2
            h = jnp.where(part_kept == 1, yh, 1 - yh)
            rows = pl.ds(pl.multiple_of(b * 256, 256), 256)
            if r == 0:
                left = full[t, 2 * x + 8 * h + b]
            else:
                left = other[t, r - 1, h, b]
            part = tn(left, act[q, r]) * factor

            @pl.when(part_kept == 1)
            def _():
                pre[q, rows] = part if first else pre[q, rows] + part

            @pl.when(part_kept == 0)
            def _():
                total = part if first else accs[rows] + part
                if last:
                    gsend[q, rows] = total.astype(BF)
                else:
                    accs[rows] = total

        if last:
            gs[q] = send(gsend.at[q], grecv.at[q], dev(dyh=1))

    def shard_rows(shard):
        return pl.ds(pl.multiple_of(shard * 256, 256), 256)

    igc = [None] * 8

    def ig_other(n, m):
        shard = 2 * m + 1 - c
        igs[m] = (
            nt(act[DGATE, 0], wi[0, shard_rows(shard)]) + nt(act[DUP, 0], wi[1, shard_rows(shard)])
        ).astype(BF)
        igc[n] = send(igs.at[m], igr.at[m], dev(dc=1))

    igzc = {}

    def ig_own(n, m):
        igc[n].wait_recv()
        shard = 2 * m + c
        total = nt(act[DGATE, 0], wi[0, shard_rows(shard)]) + nt(act[DUP, 0], wi[1, shard_rows(shard)])
        igr[m] = (total + igr[m].astype(F32)).astype(BF)

    def ig_final_1():
        for copy in igzc.values():
            copy.wait_recv()
        for y in (1, 0):
            m = chip(y, 0)
            total = igr[m].astype(F32)
            for r in range(3):
                total = total + igz[r, y].astype(F32)
            if y == 1:
                igy[0] = total.astype(BF)
                igzc["y"] = send(igy.at[0], igy.at[1], dev(dyl=1))
            else:
                pre[0, :, pl.ds(0, 256)] = total

    def ig_final_2():
        igzc["y"].wait_recv()
        ig_o[...] = (pre[0, :, pl.ds(0, 256)] + igy[1].astype(F32)).astype(BF)

    fin = 64

    def final(q):
        gs[q].wait_recv()
        if q == HID:
            col = row_out[...]
        else:
            col = col_in[pl.ds(2 - q, 1)]

        def body(i, colmax):
            rows = pl.ds(pl.multiple_of(i * fin, fin), fin)
            g = pre[q, rows] + grecv[q, rows].astype(F32)
            nu = jnp.minimum(rowv[q, rows][:, :1], col) + g * g
            upd = g * lax.rsqrt(nu)
            if q == HID:
                pre[q, rows] = upd
            else:
                upd_in_o[2 - q, rows] = upd.astype(BF)
            rowv[q, rows] = jnp.broadcast_to(jnp.max(nu, axis=1, keepdims=True), (fin, 128))
            return jnp.maximum(colmax, jnp.max(nu, axis=0, keepdims=True))

        colmax = lax.fori_loop(0, 512 // fin, body, jnp.zeros((1, h_cols), F32))
        cbuf[0, pl.ds(q, 1)] = colmax
        rbuf[0, pl.ds(q, 1), pl.ds(0, 512)] = rowv[q].T[:1]
        if q == HID:
            @pl.loop(0, h_cols // 128)
            def _(j):
                cols = pl.ds(pl.multiple_of(j * 128, 128), 128)
                upd_out_o[cols] = pre[q, :, cols].T.astype(BF)

    cbuf[0] = jnp.zeros_like(cbuf[0])
    rbuf[0] = jnp.zeros_like(rbuf[0])
    pl.semaphore_wait(barrier, len(peers))
    ag_start(0)
    for q in range(3):
        row = col_out[...] if q == HID else row_in[pl.ds(2 - q, 1)]
        rowv[q] = jnp.broadcast_to(row, (128, 512)).T
    own_tok.wait()
    own_cot.wait()
    ag_1(0)
    ag_start(1)
    for copy in load_w:
        copy.wait()
    forward(0, 0, first=True)
    ag_2a(0)
    forward(0, 3)
    forward(0, 1)
    ag_2b(0)
    forward(1, 0)
    forward(0, 2)
    ag_3(0)
    forward(1, 3)
    forward(1, 1)
    forward(1, 2)
    make_hidden()
    xg_start(HID)
    ag_1(1)
    load_wo.wait()
    backward(0, 0, first=True)
    ag_2a(1)
    backward(0, 3)
    backward(0, 1)
    ag_2b(1)
    backward(1, 0)
    backward(0, 2)
    ag_3(1)
    backward(1, 3)
    backward(1, 1)
    backward(1, 2)
    make_d()
    xg_start(DUP)
    xg_start(DGATE)
    xg_relay(HID)
    order = [(dy, dz) for dz in (2, 1, 3, 0) for dy in (1, 0)]
    for n, (dy, dz) in enumerate(order):
        ig_other(n, chip(dy, dz))
    other_share(0)
    for n, (dy, dz) in enumerate(order):
        ig_own(n, chip(dy, dz))
        if dz != 0:
            igzc[(dy, dz)] = send(igr.at[chip(dy, dz)], igz.at[dz - 1, dy], dev(dz=dz))
    other_share(1)
    other_wait(1)
    wgrad(HID, 0, first=True)
    xg_rest(HID)
    wgrad(HID, 1)
    wgrad(HID, 3)
    xg_last(HID)
    wgrad(HID, 2, last=True)
    xg_relay(DUP)
    other_wait(0)
    wgrad(DUP, 0, first=True)
    xg_rest(DUP)
    wgrad(DUP, 1)
    wgrad(DUP, 3)
    xg_relay(DGATE)
    xg_last(DUP)
    wgrad(DUP, 2, last=True)
    final(HID)
    ig_final_1()
    ig_final_2()
    wgrad(DGATE, 0, first=True)
    xg_rest(DGATE)
    wgrad(DGATE, 1)
    wgrad(DGATE, 3)
    final(DUP)
    xg_last(DGATE)
    wgrad(DGATE, 2, last=True)
    final(DGATE)

    first = [
        send(rbuf.at[0], rbuf.at[1], dev(dc=1)),
        send(rbuf.at[0], rbuf.at[2], dev(dyl=1)),
        send(rbuf.at[0], rbuf.at[3], dev(dyl=1, dc=1)),
        send(cbuf.at[0], cbuf.at[1], dev(dyh=1)),
    ]
    for copy in first:
        copy.wait_recv()
    rbuf[4] = jnp.maximum(jnp.maximum(rbuf[0], rbuf[1]), jnp.maximum(rbuf[2], rbuf[3]))
    cbuf[2] = jnp.maximum(cbuf[0], cbuf[1])
    second = []
    for r in range(1, 4):
        second.append(send(rbuf.at[4], rbuf.at[4 + r], dev(dz=r)))
        second.append(send(cbuf.at[2], cbuf.at[2 + r], dev(dx=r)))
    for copy in second:
        copy.wait_recv()
    rmax = jnp.maximum(jnp.maximum(rbuf[4], rbuf[5]), jnp.maximum(rbuf[6], rbuf[7]))
    cmax = jnp.maximum(jnp.maximum(cbuf[2], cbuf[3]), jnp.maximum(cbuf[4], cbuf[5]))
    col_out_o[...] = rmax[HID : HID + 1, :512]
    row_out_o[...] = cmax[HID : HID + 1]
    for q in (DUP, DGATE):
        row_in_o[pl.ds(2 - q, 1)] = rmax[q : q + 1, :512]
        col_in_o[pl.ds(2 - q, 1)] = cmax[q : q + 1]

    for copy in sent:
        copy.wait_send()
    for t in range(2):
        for taken, copy in xsent[t]:
            @pl.when(taken)
            def _(copy=copy):
                copy.wait_send()


def local(tokens, cotangent, w_in, w_out, row_in, col_in, row_out, col_out):
    t_rows, d_cols = tokens.shape
    h_cols = w_out.shape[0]
    factor = 1.0 / math.sqrt(t_rows * lax.axis_size("dp"))
    vmem = pl.BlockSpec(memory_space=pltpu.VMEM)
    hbm = pl.BlockSpec(memory_space=pl.ANY)
    shapes = (
        jax.ShapeDtypeStruct((t_rows, 256), BF),
        jax.ShapeDtypeStruct((2, 512, h_cols), BF),
        jax.ShapeDtypeStruct((h_cols, 512), BF),
        jax.ShapeDtypeStruct((2, 512), F32),
        jax.ShapeDtypeStruct((2, h_cols), F32),
        jax.ShapeDtypeStruct((1, h_cols), F32),
        jax.ShapeDtypeStruct((1, 512), F32),
    )
    out = pl.pallas_call(
        functools.partial(kernel, factor),
        out_shape=shapes,
        in_specs=[hbm] * 4 + [vmem] * 4,
        out_specs=[vmem] * 7,
        scratch_shapes=[
            pltpu.VMEM((2, 16, t_rows, 256), BF),
            pltpu.VMEM(w_in.shape, BF),
            pltpu.VMEM(w_out.shape, BF),
            pltpu.VMEM((3, t_rows, h_cols), F32),
            pltpu.VMEM((3, 4, t_rows, h_cols), BF),
            pltpu.VMEM((2, 3, 2, 2, t_rows, 256), BF),
            pltpu.VMEM((512, h_cols), F32),
            pltpu.VMEM((3, 512, h_cols), BF),
            pltpu.VMEM((3, 512, h_cols), BF),
            pltpu.VMEM((8, t_rows, 256), BF),
            pltpu.VMEM((8, t_rows, 256), BF),
            pltpu.VMEM((3, 2, t_rows, 256), BF),
            pltpu.VMEM((2, t_rows, 256), BF),
            pltpu.VMEM((3, 512, 128), F32),
            pltpu.VMEM((8, 8, h_cols), F32),
            pltpu.VMEM((6, 8, h_cols), F32),
            pltpu.SemaphoreType.DMA((8,)),
            pltpu.SemaphoreType.DMA((100,)),
            pltpu.SemaphoreType.DMA((100,)),
            pltpu.SemaphoreType.DMA((2, 8)),
            pltpu.SemaphoreType.DMA((2, 3, 2)),
        ],
        compiler_params=pltpu.CompilerParams(
            collective_id=0, has_side_effects=True, vmem_limit_bytes=62 * 2**20
        ),
        cost_estimate=pl.CostEstimate(
            flops=21_500_000_000, bytes_accessed=22_000_000, transcendentals=330_000
        ),
    )(
        tokens, cotangent, w_in, w_out, row_in, col_in,
        row_out.reshape(1, h_cols), col_out.reshape(1, 512),
    )
    ig, upd_in, upd_out, row_in_new, col_in_new, row_out_new, col_out_new = out
    return (
        ig, upd_in, upd_out, row_in_new, col_in_new,
        row_out_new.reshape(h_cols), col_out_new.reshape(512),
    )


def solution(mesh):
    return jax.shard_map(
        local,
        mesh=mesh,
        in_specs=(
            P("dp", "mp"),
            P("dp", "mp"),
            P(None, None, "mp"),
            P("mp", None),
            P(None, "dp"),
            P(None, "mp"),
            P("mp"),
            P("dp"),
        ),
        out_specs=(
            P("dp", "mp"),
            P(None, "dp", "mp"),
            P("mp", "dp"),
            P(None, "dp"),
            P(None, "mp"),
            P("mp"),
            P("dp"),
        ),
        check_vma=False,
    )
```

time: 398 us -> 201 us (0.51)
  waiting for transfers between devices: 250 us -> 0 us
  Pallas kernels: 0 us -> 186 us
  blocking collectives: 68.4 us -> 0 us
  matrix products: 43.8 us -> 0 us
  other arithmetic: 16.1 us -> 1.29 us
  between operations: 13.9 us -> 0.64 us
  local copies, waits for them, and re-layouts: 4.87 us -> 11.2 us
    pallas_call x0 -> x1, Pallas kernels: none -> 186 us  [local(): pl.pallas_call(functools.partial(kernel, factor), out_shape=shapes, in_sp...]
    reduce_scatter x2 -> x0, waiting for transfers between devices: 166 us -> none  [the longest x1 166 us: local(): lax.psum_scatter((jnp.stack([first, second, third], axis=1) * factor).ast...]
    all_gather x2 -> x0, waiting for transfers between devices: 83.2 us -> none  [the longest x1 48.9 us: local(): lax.all_gather(tokens, 'mp', axis=1, tiled=True)]
    pmax x2 -> x0, blocking collectives: 68.4 us -> none  [the longest x1 38.9 us: local(): col_max = lax.pmax(col_local, 'dp')]
    dot_general x8 -> x0, matrix products: 43.8 us -> none  [the longest x6 31 us: contract(): lax.dot_general(left, right, (((left_dim,), (right_dim,)), ((), ())), pre...]
    convert_element_type x2 -> x0, other arithmetic: 13.9 us -> none  [the longest x1 11.8 us: local(): (jnp.stack([first, second, third], axis=1) * factor).astype(jnp.bfloat16)]
    unnamed x21 -> x6, local copies, waits for them, and re-layouts: 2.49 us -> 9.92 us
  transfers between devices with their start and end apart: 4 -> 0, of which waited for: 3 -> 0; matrix products, arithmetic and copies ran while one was open for 9% -> 0% of each run, Pallas kernels for 0% -> 0%
where the time goes in v1:
time: 201 us; the launch traced here: 199 us
  Pallas kernels  186 us (93%)
  local copies, waits for them, and re-layouts  11.2 us (6%)
    pallas_call x1, Pallas kernels, local(): pl.pallas_call(functools.partial(kernel, factor), out_shape=shapes, in_sp...  186 us
    unnamed x6, local copies, waits for them, and re-layouts  9.92 us

profile of v1, /device:TPU:0, one launch (start us, length us, event | category | flops | bytes accessed | tf_op | source)
XLA Modules:
  0.0 198.8 jit_solution(15145628483657561362)
XLA Ops:
  0.6 1.3 reshape.26.row_out
  1.9 185.7 %shard_map.135 = (bf16[512,256]{1,0:T(8,128)(2,1)}, bf16[2,512,640]{2,1,0:T(8,128)(2,1)}, bf16[640,512]{1,0:T(8,128)(2,1)}, f32[2,512]{1,0:T(2,128)}, f32[2,640]...) custom-call(bf16[512,256]{1,0:T(8,128)(2,1)} %tok_in.1, bf16[512,256]{1,0:T(8,128)(2,1)} %cot_in.1, ...), custom_call_target="tpu_custom_call" | custom-call | flops 21500000256 | bytes 22000000 | tf_op jit(solution)/shard_map/pallas_call | solution.py:510
  187.6 1.3 reduce
  188.9 1.7 copy.21
  190.6 2.5 %copy.22 = bf16[2,512,640]{2,1,0:T(8,128)(2,1)} copy(bf16[2,512,640]{2,1,0:T(8,128)(2,1)} %get-tuple-element.29) | data formatting | bytes 2621440
  193.0 2.0 copy.23
  195.0 1.3 copy.24
  196.3 1.3 copy.25
  197.6 1.3 copy.26

commit v2 on v1

v2 whole, which is shorter than its diff:
```python
import functools
import math

import jax
import jax.numpy as jnp
from jax import lax
from jax.experimental import pallas as pl
from jax.experimental.pallas import tpu as pltpu
from jax.sharding import PartitionSpec as P

BF = jnp.bfloat16
F32 = jnp.float32
MESH = pl.DeviceIdType.MESH
ROOT = math.sqrt(2.0 / math.pi)

HID, DUP, DGATE = 0, 1, 2
PIECES = ((HID, 0, 640), (DUP, 0, 640), (DGATE, 0, 384), (DGATE, 384, 256))


def nn(a, b):
    return jnp.dot(a, b, preferred_element_type=F32)


def nt(a, b):
    return lax.dot_general(a, b, (((1,), (1,)), ((), ())), preferred_element_type=F32)


def tn(a, b):
    return lax.dot_general(a, b, (((0,), (0,)), ((), ())), preferred_element_type=F32)


def kernel(
    factor,
    tok_in,
    cot_in,
    w_in,
    w_out,
    row_in,
    col_in,
    row_out,
    col_out,
    ig_o,
    upd_in_o,
    upd_out_o,
    rmax_o,
    cmax_o,
    full,
    wi,
    wo,
    pre,
    act,
    other,
    accs,
    gsend,
    grecv,
    igs,
    igr,
    igz,
    igy,
    rowv,
    rowm,
    rbuf,
    cbuf,
    lsem,
    ssem,
    rsem,
    xssem,
    xrsem,
):
    dp, mp = lax.axis_index("dp"), lax.axis_index("mp")
    yh, x = dp // 4, dp % 4
    yl, z, c = mp // 8, (mp // 2) % 4, mp % 2
    t_rows, h_cols = pre.shape[1], pre.shape[2]
    half = t_rows // 2

    def dev(dx=0, dyh=0, dyl=0, dz=0, dc=0):
        return (
            lax.rem(yh + dyh, 2) * 4 + lax.rem(x + dx, 4),
            lax.rem(yl + dyl, 2) * 8 + lax.rem(z + dz, 4) * 2 + lax.rem(c + dc, 2),
        )

    def chip(dy, dz):
        return lax.rem(yl + dy, 2) * 4 + lax.rem(z + dz, 4)

    peers = [
        dev(dz=1), dev(dz=3), dev(dz=2), dev(dyl=1), dev(dc=1), dev(dyl=1, dc=1),
        dev(dx=1), dev(dx=3), dev(dx=2), dev(dyh=1),
    ]
    barrier = pltpu.get_barrier_semaphore()
    for peer in peers:
        pl.semaphore_signal(barrier, inc=1, device_id=peer, device_id_type=MESH)

    loads = []

    def load(src, dst):
        copy = pltpu.make_async_copy(src, dst, lsem.at[len(loads)])
        copy.start()
        loads.append(copy)
        return copy

    own_tok = load(tok_in, full.at[0, yl, z * 2 + c])
    own_cot = load(cot_in, full.at[1, yl, z * 2 + c])
    load_w = [load(w_in.at[0], wi.at[0]), load(w_in.at[1], wi.at[1])]
    load_wo = load(w_out, wo)

    sent = []

    def send(src, dst, device):
        i = len(sent)
        copy = pltpu.make_async_remote_copy(
            src_ref=src, dst_ref=dst, send_sem=ssem.at[i], recv_sem=rsem.at[i],
            device_id=device, device_id_type=MESH,
        )
        copy.start()
        sent.append(copy)
        return copy

    xsent = [[], []]

    def xsend(t, dy, dz, src):
        origin_z = lax.rem(z + dz, 4)
        origin_y = lax.rem(yl + dy, 2)
        dx = lax.rem(origin_z + 4 - x, 4)
        there = dx // 2 * 2
        i = len(xsent[t])
        copy = pltpu.make_async_remote_copy(
            src_ref=src,
            dst_ref=other.at[t, there, origin_y, c],
            send_sem=xssem.at[t, i], recv_sem=xrsem.at[t, there // 2, origin_y],
            device_id=(yh * 4 + origin_z, mp), device_id_type=MESH,
        )
        xsent[t].append((dx % 2 == 1, copy))

        @pl.when(dx % 2 == 1)
        def _():
            copy.start()

    sib = [{}, {}]

    class Gather:
        def __init__(self, slot, share):
            self.slot, self.share, self.got = slot, share, {}

        def push(self, name, dy, dz, part, device, src=None):
            slot = self.slot(dy, dz, part)
            self.got[name] = send(slot if src is None else src, slot, device)

        def start(self, src=None):
            self.push("z-", 0, 0, None, dev(dz=1), src)
            self.push("z+", 0, 0, None, dev(dz=3), src)
            self.push("y", 0, 0, None, dev(dyl=1), src)
            self.share(0, 0, src)

        def one(self):
            self.got["z-"].wait_recv()
            self.push("zz-", 0, 3, 0, dev(dz=1))
            self.share(0, 3, None)
            self.got["z+"].wait_recv()
            self.push("zz+", 0, 1, 1, dev(dz=3))
            self.share(0, 1, None)
            self.got["y"].wait_recv()
            self.push("yz-", 1, 0, None, dev(dz=1))
            self.push("yz+", 1, 0, None, dev(dz=3))
            self.share(1, 0, None)

        def two(self):
            self.got["zz-"].wait_recv()
            self.push("yzz-", 0, 2, 0, dev(dyl=1))
            self.got["zz+"].wait_recv()
            self.push("yzz+", 0, 2, 1, dev(dyl=1))
            self.share(0, 2, None)

        def three(self):
            self.got["yz-"].wait_recv()
            self.share(1, 3, None)
            self.got["yz+"].wait_recv()
            self.share(1, 1, None)

        def four(self):
            self.got["yzz-"].wait_recv()
            self.got["yzz+"].wait_recv()
            self.share(1, 2, None)

    def full_gather(t):
        def slot(dy, dz, part):
            ref = full.at[t, lax.rem(yl + dy, 2), lax.rem(z + dz, 4) * 2 + c]
            return ref if part is None else ref.at[pl.ds(part * half, half)]

        def share(dy, dz, src):
            ref = slot(dy, dz, None)
            sib[t][(dy, dz)] = send(ref if src is None else src, ref, dev(dc=1))
            xsend(t, dy, dz, ref if src is None else src)

        return Gather(slot, share)

    e2_rows = t_rows // 8

    def e2_slot(dy, dz, part):
        m = chip(dy, dz)
        if part is None:
            rows = pl.ds(pl.multiple_of(m * e2_rows, e2_rows), e2_rows)
        else:
            rows = pl.ds(
                pl.multiple_of(m * e2_rows + part * (e2_rows // 2), e2_rows // 2), e2_rows // 2
            )
        return other.at[:, 1, :, c, rows]

    ga, gb, ge = full_gather(0), full_gather(1), Gather(e2_slot, lambda dy, dz, src: None)
    e2 = []

    def e2_send():
        rows = pl.ds(pl.multiple_of(chip(0, 0) * e2_rows, e2_rows), e2_rows)
        e2.append(
            send(
                full.at[:, :, lax.rem(x + 2, 4) * 2 + c, rows],
                other.at[:, 1, :, c, rows],
                dev(dx=2),
            )
        )

    def e2_start():
        e2[0].wait_recv()
        ge.start()

    def forward(dy, dz, first=False):
        sib[0][(dy, dz)].wait_recv()
        m = chip(dy, dz)
        my, mz = lax.rem(yl + dy, 2), lax.rem(z + dz, 4) * 2

        @pl.loop(0, 4)
        def _(i):
            k, rows = i // 2, pl.ds(pl.multiple_of((i % 2) * half, half), half)
            part = nn(full[0, my, mz, rows], wi[k, pl.ds(pl.multiple_of(m * 512, 512), 256)]) + nn(
                full[0, my, mz + 1, rows], wi[k, pl.ds(pl.multiple_of(m * 512 + 256, 256), 256)]
            )
            if first:
                pre[k, rows] = part
            else:
                pre[k, rows] += part

    def backward(dy, dz, first=False):
        sib[1][(dy, dz)].wait_recv()
        m = chip(dy, dz)
        my, mz = lax.rem(yl + dy, 2), lax.rem(z + dz, 4) * 2

        @pl.loop(0, 2)
        def _(i):
            rows = pl.ds(pl.multiple_of(i * half, half), half)
            part = nt(full[1, my, mz, rows], wo[:, pl.ds(pl.multiple_of(m * 512, 512), 256)]) + nt(
                full[1, my, mz + 1, rows], wo[:, pl.ds(pl.multiple_of(m * 512 + 256, 256), 256)]
            )
            if first:
                pre[2, rows] = part
            else:
                pre[2, rows] += part

    step = 32

    def make_hidden():
        @pl.loop(0, t_rows // step)
        def _(i):
            rows = pl.ds(pl.multiple_of(i * step, step), step)
            v = pre[0, rows]
            up = pre[1, rows]
            t = jnp.tanh(ROOT * (v + 0.044715 * v * v * v))
            activated = 0.5 * v * (1.0 + t)
            slopes = 0.5 * (1.0 + t) + 0.5 * v * (1.0 - t * t) * ROOT * (
                1.0 + 3.0 * 0.044715 * v * v
            )
            act[HID, 0, rows] = (activated * up).astype(BF)
            pre[0, rows] = activated
            pre[1, rows] = up * slopes

    def make_d():
        @pl.loop(0, t_rows // step)
        def _(i):
            rows = pl.ds(pl.multiple_of(i * step, step), step)
            d = pre[2, rows]
            act[DUP, 0, rows] = (d * pre[0, rows]).astype(BF)
            act[DGATE, 0, rows] = (d * pre[1, rows]).astype(BF)

    xg = [{} for _ in PIECES]
    lo, hi = pl.ds(0, half), pl.ds(half, half)

    def xg_send(p, name, source, there, rows, device):
        q, first_col, cols = PIECES[p]
        cut = pl.ds(first_col, cols)
        xg[p][name] = send(act.at[q, source, rows, cut], act.at[q, there, rows, cut], device)

    def xg_start(p):
        xg_send(p, "a-", 0, 1, lo, dev(dx=1))
        xg_send(p, "b+", 0, 3, hi, dev(dx=3))
        xg_send(p, "b-", 0, 1, hi, dev(dx=1))
        xg_send(p, "a+", 0, 3, lo, dev(dx=3))

    def xg_relay(p):
        xg[p]["a-"].wait_recv()
        xg_send(p, "aa", 1, 2, lo, dev(dx=1))
        xg[p]["b+"].wait_recv()
        xg_send(p, "bb", 3, 2, hi, dev(dx=3))

    def xg_rest(p):
        xg[p]["b-"].wait_recv()
        xg[p]["a+"].wait_recv()

    def xg_last(p):
        xg[p]["aa"].wait_recv()
        xg[p]["bb"].wait_recv()

    osib = [[], []]

    def other_share(t):
        for r in (0, 2):
            for h in range(2):
                slot = other.at[t, r, h, c]
                pltpu.make_async_remote_copy(
                    src_ref=slot, dst_ref=slot, send_sem=xssem.at[t, 0],
                    recv_sem=xrsem.at[t, r // 2, h], device_id=dev(dc=1), device_id_type=MESH,
                ).wait_recv()
            slot = other.at[t, r, :, c]
            osib[t].append(send(slot, slot, dev(dc=1)))

    def e2_share():
        slot = other.at[:, 1, :, c]
        e2.append(send(slot, slot, dev(dc=1)))

    def other_wait(t):
        for copy in osib[t]:
            copy.wait_recv()

    def e2_wait():
        e2[1].wait_recv()

    gs = [None] * len(PIECES)

    def wgrad(p, r, first=False, last=False):
        q, first_col, n = PIECES[p]
        cut = pl.ds(first_col, n)
        t = 1 if q == HID else 0

        @pl.loop(0, 4)
        def _(i):
            part_kept, b = i // 2, i % 2
            h = jnp.where(part_kept == 1, yh, 1 - yh)
            rows = pl.ds(pl.multiple_of(b * 256, 256), 256)
            if r == 0:
                left = full[t, h, 2 * x + b]
            else:
                left = other[t, r - 1, h, b]
            part = tn(left, act[q, r, :, cut]) * factor

            @pl.when(part_kept == 1)
            def _():
                pre[q, rows, cut] = part if first else pre[q, rows, cut] + part

            @pl.when(part_kept == 0)
            def _():
                total = part if first else accs[rows, cut] + part
                if last:
                    gsend[q, rows, cut] = total.astype(BF)
                else:
                    accs[rows, cut] = total

        if last:
            gs[p] = send(gsend.at[q, :, cut], grecv.at[q, :, cut], dev(dyh=1))

    def shard_rows(shard):
        return pl.ds(pl.multiple_of(shard * 256, 256), 256)

    igc = [None] * 8

    def ig_other(n, m):
        shard = 2 * m + 1 - c
        igs[m] = (
            nt(act[DGATE, 0], wi[0, shard_rows(shard)]) + nt(act[DUP, 0], wi[1, shard_rows(shard)])
        ).astype(BF)
        igc[n] = send(igs.at[m], igr.at[m], dev(dc=1))

    igzc = {}

    def ig_own(n, m):
        igc[n].wait_recv()
        shard = 2 * m + c
        total = nt(act[DGATE, 0], wi[0, shard_rows(shard)]) + nt(act[DUP, 0], wi[1, shard_rows(shard)])
        igr[m] = (total + igr[m].astype(F32)).astype(BF)

    def ig_final_1():
        for copy in igzc.values():
            copy.wait_recv()
        for y in (1, 0):
            m = chip(y, 0)
            total = igr[m].astype(F32)
            for r in range(3):
                total = total + igz[r, y].astype(F32)
            if y == 1:
                igy[0] = total.astype(BF)
                igzc["y"] = send(igy.at[0], igy.at[1], dev(dyl=1))
            else:
                pre[0, :, pl.ds(0, 256)] = total

    def ig_final_2():
        igzc["y"].wait_recv()
        ig_o[...] = (pre[0, :, pl.ds(0, 256)] + igy[1].astype(F32)).astype(BF)

    fin = 64

    def final(p):
        q, first_col, n = PIECES[p]
        cut = pl.ds(first_col, n)
        gs[p].wait_recv()
        col = row_out[...].reshape(1, h_cols) if q == HID else col_in[pl.ds(2 - q, 1), cut]

        def body(i, colmax):
            rows = pl.ds(pl.multiple_of(i * fin, fin), fin)
            g = pre[q, rows, cut] + grecv[q, rows, cut].astype(F32)
            nu = jnp.minimum(rowv[q, rows][:, :1], col) + g * g
            upd = g * lax.rsqrt(nu)
            if q == HID:
                pre[q, rows] = upd
            else:
                upd_in_o[2 - q, rows, cut] = upd.astype(BF)
            rowm[p, rows] = jnp.broadcast_to(jnp.max(nu, axis=1, keepdims=True), (fin, 128))
            return jnp.maximum(colmax, jnp.max(nu, axis=0, keepdims=True))

        colmax = lax.fori_loop(0, 512 // fin, body, jnp.zeros((1, n), F32))
        cbuf[0, pl.ds(q, 1), cut] = colmax
        rowmax = rowm[p].T[:1]
        if first_col != 0:
            rowmax = jnp.maximum(rowmax, rbuf[0, pl.ds(q, 1), pl.ds(0, 512)])
        rbuf[0, pl.ds(q, 1), pl.ds(0, 512)] = rowmax
        if q == HID:
            @pl.loop(0, h_cols // 128)
            def _(j):
                cols = pl.ds(pl.multiple_of(j * 128, 128), 128)
                upd_out_o[cols] = pre[q, :, cols].T.astype(BF)

    cbuf[0] = jnp.zeros_like(cbuf[0])
    rbuf[0] = jnp.zeros_like(rbuf[0])
    pl.semaphore_wait(barrier, len(peers))
    ga.start(tok_in)
    for q in range(3):
        row = col_out[...].reshape(1, 512) if q == HID else row_in[pl.ds(2 - q, 1)]
        rowv[q] = jnp.broadcast_to(row, (128, 512)).T
    own_tok.wait()
    own_cot.wait()
    ga.one()
    gb.start(cot_in)
    for copy in load_w:
        copy.wait()
    forward(0, 0, first=True)
    ga.two()
    forward(0, 3)
    forward(0, 1)
    ga.three()
    forward(1, 0)
    forward(0, 2)
    ga.four()
    forward(1, 3)
    forward(1, 1)
    forward(1, 2)
    make_hidden()
    xg_start(0)
    gb.one()
    load_wo.wait()
    backward(0, 0, first=True)
    gb.two()
    backward(0, 3)
    backward(0, 1)
    gb.three()
    backward(1, 0)
    backward(0, 2)
    gb.four()
    e2_send()
    backward(1, 3)
    backward(1, 1)
    backward(1, 2)
    make_d()
    xg_relay(0)
    xg_start(1)
    order = [(dy, dz) for dz in (2, 1, 3, 0) for dy in (1, 0)]
    for n, (dy, dz) in enumerate(order[:4]):
        ig_other(n, chip(dy, dz))
    e2_start()
    for n, (dy, dz) in enumerate(order[4:]):
        ig_other(4 + n, chip(dy, dz))
    other_share(1)
    ge.one()
    xg_relay(1)
    xg_start(2)
    for n, (dy, dz) in enumerate(order):
        ig_own(n, chip(dy, dz))
        if dz != 0:
            igzc[(dy, dz)] = send(igr.at[chip(dy, dz)], igz.at[dz - 1, dy], dev(dz=dz))
        if n == 3:
            ge.two()
    ge.three()
    ge.four()
    e2_share()
    other_share(0)
    other_wait(1)
    wgrad(0, 0, first=True)
    xg_rest(0)
    wgrad(0, 1)
    wgrad(0, 3)
    xg_last(0)
    e2_wait()
    wgrad(0, 2, last=True)
    other_wait(0)
    wgrad(1, 0, first=True)
    xg_rest(1)
    wgrad(1, 1)
    wgrad(1, 3)
    xg_relay(2)
    xg_start(3)
    xg_last(1)
    wgrad(1, 2, last=True)
    final(0)
    ig_final_1()
    wgrad(2, 0, first=True)
    xg_rest(2)
    wgrad(2, 1)
    wgrad(2, 3)
    xg_relay(3)
    xg_last(2)
    wgrad(2, 2, last=True)
    ig_final_2()
    final(1)
    wgrad(3, 0, first=True)
    xg_rest(3)
    wgrad(3, 1)
    wgrad(3, 3)
    xg_last(3)
    wgrad(3, 2, last=True)
    final(2)
    final(3)

    first = [
        send(rbuf.at[0], rbuf.at[1], dev(dc=1)),
        send(rbuf.at[0], rbuf.at[2], dev(dyl=1)),
        send(rbuf.at[0], rbuf.at[3], dev(dyl=1, dc=1)),
        send(cbuf.at[0], cbuf.at[1], dev(dyh=1)),
    ]
    for copy in first:
        copy.wait_recv()
    rbuf[4] = jnp.maximum(jnp.maximum(rbuf[0], rbuf[1]), jnp.maximum(rbuf[2], rbuf[3]))
    cbuf[2] = jnp.maximum(cbuf[0], cbuf[1])
    second = []
    for r in range(1, 4):
        second.append(send(rbuf.at[4], rbuf.at[4 + r], dev(dz=r)))
        second.append(send(cbuf.at[2], cbuf.at[2 + r], dev(dx=r)))
    for copy in second:
        copy.wait_recv()
    rmax_o[...] = jnp.maximum(jnp.maximum(rbuf[4], rbuf[5]), jnp.maximum(rbuf[6], rbuf[7]))
    cmax_o[...] = jnp.maximum(jnp.maximum(cbuf[2], cbuf[3]), jnp.maximum(cbuf[4], cbuf[5]))

    for copy in sent:
        copy.wait_send()
    for t in range(2):
        for taken, copy in xsent[t]:
            @pl.when(taken)
            def _(copy=copy):
                copy.wait_send()


def finish(
    ig, upd_in, upd_out, rmax, cmax,
    ig_o, upd_in_o, upd_out_o, row_in_o, col_in_o, row_out_o, col_out_o,
    ig_v, upd_in_v, upd_out_v, sem,
):
    steps = ((ig, ig_v, ig_o), (upd_in, upd_in_v, upd_in_o), (upd_out, upd_out_v, upd_out_o))
    ins = [pltpu.make_async_copy(s, v, sem.at[0, i]) for i, (s, v, o) in enumerate(steps)]
    copies = [pltpu.make_async_copy(v, o, sem.at[1, i]) for i, (s, v, o) in enumerate(steps)]
    for copy in ins:
        copy.start()
    n = row_in_o.shape[1]
    col_out_o[...] = rmax[HID, pl.ds(0, n)]
    row_out_o[...] = cmax[HID]
    for q in (DUP, DGATE):
        row_in_o[pl.ds(2 - q, 1)] = rmax[q : q + 1, :n]
        col_in_o[pl.ds(2 - q, 1)] = cmax[q : q + 1]
    for before, copy in zip(ins, copies):
        before.wait()
        copy.start()
    for copy in copies:
        copy.wait()


def local(tokens, cotangent, w_in, w_out, row_in, col_in, row_out, col_out):
    t_rows, d_cols = tokens.shape
    h_cols = w_out.shape[0]
    factor = 1.0 / math.sqrt(t_rows * lax.axis_size("dp"))
    vmem = pl.BlockSpec(memory_space=pltpu.VMEM)
    hbm = pl.BlockSpec(memory_space=pl.ANY)
    shapes = (
        jax.ShapeDtypeStruct((t_rows, 256), BF),
        jax.ShapeDtypeStruct((2, 512, h_cols), BF),
        jax.ShapeDtypeStruct((h_cols, 512), BF),
        jax.ShapeDtypeStruct((8, h_cols), F32),
        jax.ShapeDtypeStruct((8, h_cols), F32),
    )
    out = pl.pallas_call(
        functools.partial(kernel, factor),
        out_shape=shapes,
        in_specs=[hbm] * 4 + [vmem] * 4,
        out_specs=[vmem] * 5,
        scratch_shapes=[
            pltpu.VMEM((2, 2, 8, t_rows, 256), BF),
            pltpu.VMEM(w_in.shape, BF),
            pltpu.VMEM(w_out.shape, BF),
            pltpu.VMEM((3, t_rows, h_cols), F32),
            pltpu.VMEM((3, 4, t_rows, h_cols), BF),
            pltpu.VMEM((2, 3, 2, 2, t_rows, 256), BF),
            pltpu.VMEM((512, h_cols), F32),
            pltpu.VMEM((3, 512, h_cols), BF),
            pltpu.VMEM((3, 512, h_cols), BF),
            pltpu.VMEM((8, t_rows, 256), BF),
            pltpu.VMEM((8, t_rows, 256), BF),
            pltpu.VMEM((3, 2, t_rows, 256), BF),
            pltpu.VMEM((2, t_rows, 256), BF),
            pltpu.VMEM((3, 512, 128), F32),
            pltpu.VMEM((4, 512, 128), F32),
            pltpu.VMEM((8, 8, h_cols), F32),
            pltpu.VMEM((6, 8, h_cols), F32),
            pltpu.SemaphoreType.DMA((8,)),
            pltpu.SemaphoreType.DMA((140,)),
            pltpu.SemaphoreType.DMA((140,)),
            pltpu.SemaphoreType.DMA((2, 8)),
            pltpu.SemaphoreType.DMA((2, 2, 2)),
        ],
        compiler_params=pltpu.CompilerParams(
            collective_id=0, has_side_effects=True, vmem_limit_bytes=62 * 2**20
        ),
        cost_estimate=pl.CostEstimate(
            flops=21_500_000_000, bytes_accessed=22_000_000, transcendentals=330_000
        ),
    )(tokens, cotangent, w_in, w_out, row_in, col_in, row_out, col_out)
    return pl.pallas_call(
        finish,
        out_shape=shapes[:3]
        + (
            jax.ShapeDtypeStruct(row_in.shape, F32),
            jax.ShapeDtypeStruct(col_in.shape, F32),
            jax.ShapeDtypeStruct(row_out.shape, F32),
            jax.ShapeDtypeStruct(col_out.shape, F32),
        ),
        in_specs=[hbm] * 3 + [vmem] * 2,
        out_specs=[hbm] * 3 + [vmem] * 4,
        scratch_shapes=[pltpu.VMEM(s.shape, BF) for s in shapes[:3]]
        + [pltpu.SemaphoreType.DMA((2, 3))],
    )(*out)


def solution(mesh):
    return jax.shard_map(
        local,
        mesh=mesh,
        in_specs=(
            P("dp", "mp"),
            P("dp", "mp"),
            P(None, None, "mp"),
            P("mp", None),
            P(None, "dp"),
            P(None, "mp"),
            P("mp"),
            P("dp"),
        ),
        out_specs=(
            P("dp", "mp"),
            P(None, "dp", "mp"),
            P("mp", "dp"),
            P(None, "dp"),
            P(None, "mp"),
            P("mp"),
            P("dp"),
        ),
        check_vma=False,
    )
```

time: 201 us -> 165 us (0.82)
  Pallas kernels: 186 us -> 164 us
  local copies, waits for them, and re-layouts: 11.2 us -> 0 us
    pallas_call x1, Pallas kernels: 186 us -> 159 us  [local(): pl.pallas_call(functools.partial(kernel, factor), out_shape=shapes, in_sp...]
    unnamed x6 -> x0, local copies, waits for them, and re-layouts: 9.92 us -> none
    pallas_call x0 -> x1, Pallas kernels: none -> 4.07 us  [local(): pl.pallas_call(finish, out_shape=shapes[:3] + (jax.ShapeDtypeStruct(row_i...]
where the time goes in v2:
time: 165 us; the launch traced here: 164 us
  Pallas kernels  164 us (99%)
    pallas_call x1, Pallas kernels, local(): pl.pallas_call(functools.partial(kernel, factor), out_shape=shapes, in_sp...  159 us
    pallas_call x1, Pallas kernels, local(): pl.pallas_call(finish, out_shape=shapes[:3] + (jax.ShapeDtypeStruct(row_i...  4.07 us

profile of v2, /device:TPU:0, one launch (start us, length us, event | category | flops | bytes accessed | tf_op | source)
XLA Modules:
  0.0 164.3 jit_solution(8972434433780253414)
XLA Ops:
  0.6 159.5 %shard_map.135 = (bf16[512,256]{1,0:T(8,128)(2,1)}, bf16[2,512,640]{2,1,0:T(8,128)(2,1)}, bf16[640,512]{1,0:T(8,128)(2,1)}, f32[8,640]{1,0:T(8,128)}, f32[8,640]{1,0:T(8,128)}) custom-call(bf16[512,256]{1,0:T(8,128)(2,1)} %tok_in.1, bf16[512,256]{1,0:T(8,128)(2,1)} %cot_in.1, bf16[2,4096,640]{2,1,0:T(8,128)(2,1)} %w_in.1, bf16[640,4096]{1,0:T(8,128)(2,1)} %w_out.1, ...), custom_call_target="tpu_custom_call" | custom-call | flops 21500000256 | bytes 22000000 | tf_op jit(solution)/shard_map/pallas_call | solution.py:601
  160.1 4.1 %shard_map.136 = (bf16[512,256]{1,0:T(8,128)(2,1)}, bf16[2,512,640]{2,1,0:T(8,128)(2,1)}, bf16[640,512]{1,0:T(8,128)(2,1)}, f32[2,512]{1,0:T(2,128)}, f32[2,640]{1,0:T(2,128)}, /*index=5*/f32[640]{0:T(1024)}, f32[512]{0:T(512)}) custom-call(bf16[512,256]{1,0:T(8,128)(2,1)} %get-tuple-element.12.ig, bf16[2,512,640]{2,1,0:T(8,128)(2,1)} %get-tuple-element.13.upd_in, ...), custom_call_target="tpu_custom_call" | custom-call | tf_op jit(solution)/shard_map/pallas_call | solution.py:637

commit v3 on v2

--- a/solution.py
+++ b/solution.py
@@ -14,6 +14,8 @@
 ROOT = math.sqrt(2.0 / math.pi)
 
 HID, DUP, DGATE = 0, 1, 2
+MESSAGES = 133
+SENDING = 48
 PIECES = ((HID, 0, 640), (DUP, 0, 640), (DGATE, 0, 384), (DGATE, 384, 256))
 
 
@@ -39,9 +41,9 @@
     col_in,
     row_out,
     col_out,
-    ig_o,
-    upd_in_o,
-    upd_out_o,
+    ig_h,
+    upd_in_h,
+    upd_out_h,
     rmax_o,
     cmax_o,
     full,
@@ -61,6 +63,9 @@
     rowm,
     rbuf,
     cbuf,
+    ig_o,
+    upd_in_o,
+    upd_out_o,
     lsem,
     ssem,
     rsem,
@@ -100,36 +105,36 @@
 
     own_tok = load(tok_in, full.at[0, yl, z * 2 + c])
     own_cot = load(cot_in, full.at[1, yl, z * 2 + c])
-    load_w = [load(w_in.at[0], wi.at[0]), load(w_in.at[1], wi.at[1])]
-    load_wo = load(w_out, wo)
 
     sent = []
 
     def send(src, dst, device):
         i = len(sent)
+        if i >= SENDING:
+            sent[i - SENDING].wait_send()
         copy = pltpu.make_async_remote_copy(
-            src_ref=src, dst_ref=dst, send_sem=ssem.at[i], recv_sem=rsem.at[i],
+            src_ref=src, dst_ref=dst, send_sem=ssem.at[i % SENDING], recv_sem=rsem.at[i],
             device_id=device, device_id_type=MESH,
         )
         copy.start()
         sent.append(copy)
         return copy
 
-    xsent = [[], []]
-
-    def xsend(t, dy, dz, src):
+    xsent = []
+
+    def xsend(dy, dz, src):
         origin_z = lax.rem(z + dz, 4)
         origin_y = lax.rem(yl + dy, 2)
         dx = lax.rem(origin_z + 4 - x, 4)
         there = dx // 2 * 2
-        i = len(xsent[t])
+        i = len(xsent)
         copy = pltpu.make_async_remote_copy(
             src_ref=src,
-            dst_ref=other.at[t, there, origin_y, c],
-            send_sem=xssem.at[t, i], recv_sem=xrsem.at[t, there // 2, origin_y],
+            dst_ref=other.at[0, there, origin_y, c],
+            send_sem=xssem.at[i], recv_sem=xrsem.at[there // 2, origin_y],
             device_id=(yh * 4 + origin_z, mp), device_id_type=MESH,
         )
-        xsent[t].append((dx % 2 == 1, copy))
+        xsent.append((dx % 2 == 1, copy))
 
         @pl.when(dx % 2 == 1)
         def _():
@@ -143,42 +148,59 @@
 
         def push(self, name, dy, dz, part, device, src=None):
             slot = self.slot(dy, dz, part)
-            self.got[name] = send(slot if src is None else src, slot, device)
+            self.got[name] = send(slot if src is None else self.part_of(src, part), slot, device)
+
+        def part_of(self, src, part):
+            n = src.shape[0] // 2
+            return src.at[pl.ds(part * n, n)]
+
+        def wait(self, name):
+            self.got[name].wait_recv()
 
         def start(self, src=None):
-            self.push("z-", 0, 0, None, dev(dz=1), src)
-            self.push("z+", 0, 0, None, dev(dz=3), src)
-            self.push("y", 0, 0, None, dev(dyl=1), src)
+            self.push("z-0", 0, 0, 0, dev(dz=1), src)
+            self.push("z+1", 0, 0, 1, dev(dz=3), src)
+            self.push("y0", 0, 0, 0, dev(dyl=1), src)
+            self.push("z-1", 0, 0, 1, dev(dz=1), src)
+            self.push("z+0", 0, 0, 0, dev(dz=3), src)
+            self.push("y1", 0, 0, 1, dev(dyl=1), src)
             self.share(0, 0, src)
 
         def one(self):
-            self.got["z-"].wait_recv()
-            self.push("zz-", 0, 3, 0, dev(dz=1))
+            self.wait("z-0")
+            self.push("zz0", 0, 3, 0, dev(dz=1))
+            self.wait("z+1")
+            self.push("zz1", 0, 1, 1, dev(dz=3))
+            self.wait("y0")
+            self.push("yz-0", 1, 0, 0, dev(dz=1))
+            self.push("yz+0", 1, 0, 0, dev(dz=3))
+            self.wait("z-1")
             self.share(0, 3, None)
-            self.got["z+"].wait_recv()
-            self.push("zz+", 0, 1, 1, dev(dz=3))
+            self.wait("z+0")
             self.share(0, 1, None)
-            self.got["y"].wait_recv()
-            self.push("yz-", 1, 0, None, dev(dz=1))
-            self.push("yz+", 1, 0, None, dev(dz=3))
+            self.wait("y1")
+            self.push("yz-1", 1, 0, 1, dev(dz=1))
+            self.push("yz+1", 1, 0, 1, dev(dz=3))
             self.share(1, 0, None)
 
         def two(self):
-            self.got["zz-"].wait_recv()
-            self.push("yzz-", 0, 2, 0, dev(dyl=1))
-            self.got["zz+"].wait_recv()
-            self.push("yzz+", 0, 2, 1, dev(dyl=1))
+            self.wait("zz0")
+            self.push("yzz0", 0, 2, 0, dev(dyl=1))
+            self.wait("zz1")
+            self.push("yzz1", 0, 2, 1, dev(dyl=1))
             self.share(0, 2, None)
 
         def three(self):
-            self.got["yz-"].wait_recv()
+            self.wait("yz-0")
+            self.wait("yz-1")
             self.share(1, 3, None)
-            self.got["yz+"].wait_recv()
+            self.wait("yz+0")
+            self.wait("yz+1")
             self.share(1, 1, None)
 
         def four(self):
-            self.got["yzz-"].wait_recv()
-            self.got["yzz+"].wait_recv()
+            self.wait("yzz0")
+            self.wait("yzz1")
             self.share(1, 2, None)
 
     def full_gather(t):
@@ -189,38 +211,50 @@
         def share(dy, dz, src):
             ref = slot(dy, dz, None)
             sib[t][(dy, dz)] = send(ref if src is None else src, ref, dev(dc=1))
-            xsend(t, dy, dz, ref if src is None else src)
+            if t == 0:
+                xsend(dy, dz, ref if src is None else src)
 
         return Gather(slot, share)
 
     e2_rows = t_rows // 8
-
-    def e2_slot(dy, dz, part):
-        m = chip(dy, dz)
-        if part is None:
-            rows = pl.ds(pl.multiple_of(m * e2_rows, e2_rows), e2_rows)
-        else:
-            rows = pl.ds(
-                pl.multiple_of(m * e2_rows + part * (e2_rows // 2), e2_rows // 2), e2_rows // 2
+    far = ((1, 1), (0, 3))
+
+    def e2_gather(t):
+        first, count = far[t]
+
+        def slot(dy, dz, part):
+            n = e2_rows // 2
+            rows = pl.ds(pl.multiple_of(chip(dy, dz) * e2_rows + part * n, n), n)
+            return other.at[t, pl.ds(first, count), :, c, rows]
+
+        return Gather(slot, lambda dy, dz, src: None)
+
+    ga, gb = full_gather(0), full_gather(1)
+    ge = [e2_gather(0), e2_gather(1)]
+    e2 = [[], []]
+    eshare = [None, None]
+
+    def e2_send(t):
+        rows = pl.ds(pl.multiple_of(chip(0, 0) * e2_rows, e2_rows), e2_rows)
+        first, count = far[t]
+        for r in range(first, first + count):
+            e2[t].append(
+                send(
+                    full.at[t, :, lax.rem(x + r + 1, 4) * 2 + c, rows],
+                    other.at[t, r, :, c, rows],
+                    dev(dx=r + 1),
+                )
             )
-        return other.at[:, 1, :, c, rows]
-
-    ga, gb, ge = full_gather(0), full_gather(1), Gather(e2_slot, lambda dy, dz, src: None)
-    e2 = []
-
-    def e2_send():
-        rows = pl.ds(pl.multiple_of(chip(0, 0) * e2_rows, e2_rows), e2_rows)
-        e2.append(
-            send(
-                full.at[:, :, lax.rem(x + 2, 4) * 2 + c, rows],
-                other.at[:, 1, :, c, rows],
-                dev(dx=2),
-            )
-        )
-
-    def e2_start():
-        e2[0].wait_recv()
-        ge.start()
+
+    def e2_start(t):
+        for copy in e2[t]:
+            copy.wait_recv()
+        ge[t].start()
+
+    def e2_share(t):
+        first, count = far[t]
+        slot = other.at[t, pl.ds(first, count), :, c]
+        eshare[t] = send(slot, slot, dev(dc=1))
 
     def forward(dy, dz, first=False):
         sib[0][(dy, dz)].wait_recv()
@@ -307,29 +341,24 @@
         xg[p]["aa"].wait_recv()
         xg[p]["bb"].wait_recv()
 
-    osib = [[], []]
-
-    def other_share(t):
+    osib = []
+
+    def other_share():
         for r in (0, 2):
             for h in range(2):
-                slot = other.at[t, r, h, c]
+                slot = other.at[0, r, h, c]
                 pltpu.make_async_remote_copy(
-                    src_ref=slot, dst_ref=slot, send_sem=xssem.at[t, 0],
-                    recv_sem=xrsem.at[t, r // 2, h], device_id=dev(dc=1), device_id_type=MESH,
+                    src_ref=slot, dst_ref=slot, send_sem=xssem.at[0],
+                    recv_sem=xrsem.at[r // 2, h], device_id=dev(dc=1), device_id_type=MESH,
                 ).wait_recv()
-            slot = other.at[t, r, :, c]
-            osib[t].append(send(slot, slot, dev(dc=1)))
-
-    def e2_share():
-        slot = other.at[:, 1, :, c]
-        e2.append(send(slot, slot, dev(dc=1)))
+            slot = other.at[0, r, :, c]
+            osib.append(send(slot, slot, dev(dc=1)))
 
     def other_wait(t):
-        for copy in osib[t]:
-            copy.wait_recv()
-
-    def e2_wait():
-        e2[1].wait_recv()
+        eshare[t].wait_recv()
+        if t == 0:
+            for copy in osib:
+                copy.wait_recv()
 
     gs = [None] * len(PIECES)
 
@@ -396,11 +425,13 @@
                 igy[0] = total.astype(BF)
                 igzc["y"] = send(igy.at[0], igy.at[1], dev(dyl=1))
             else:
-                pre[0, :, pl.ds(0, 256)] = total
+                rowm[2], rowm[3] = total[:, :128], total[:, 128:]
 
     def ig_final_2():
         igzc["y"].wait_recv()
-        ig_o[...] = (pre[0, :, pl.ds(0, 256)] + igy[1].astype(F32)).astype(BF)
+        for i in range(2):
+            cols = pl.ds(i * 128, 128)
+            ig_o[:, cols] = (rowm[2 + i] + igy[1, :, cols].astype(F32)).astype(BF)
 
     fin = 64
 
@@ -434,10 +465,11 @@
                 cols = pl.ds(pl.multiple_of(j * 128, 128), 128)
                 upd_out_o[cols] = pre[q, :, cols].T.astype(BF)
 
+    pl.semaphore_wait(barrier, len(peers))
+    ga.start(tok_in)
+    load_w = [load(w_in.at[0], wi.at[0]), load(w_in.at[1], wi.at[1])]
     cbuf[0] = jnp.zeros_like(cbuf[0])
     rbuf[0] = jnp.zeros_like(rbuf[0])
-    pl.semaphore_wait(barrier, len(peers))
-    ga.start(tok_in)
     for q in range(3):
         row = col_out[...].reshape(1, 512) if q == HID else row_in[pl.ds(2 - q, 1)]
         rowv[q] = jnp.broadcast_to(row, (128, 512)).T
@@ -445,16 +477,18 @@
     own_cot.wait()
     ga.one()
     gb.start(cot_in)
+    load_wo = load(w_out, wo)
+    ga.two()
     for copy in load_w:
         copy.wait()
     forward(0, 0, first=True)
-    ga.two()
     forward(0, 3)
     forward(0, 1)
     ga.three()
     forward(1, 0)
+    ga.four()
+    e2_send(0)
     forward(0, 2)
-    ga.four()
     forward(1, 3)
     forward(1, 1)
     forward(1, 2)
@@ -464,75 +498,87 @@
     load_wo.wait()
     backward(0, 0, first=True)
     gb.two()
+    e2_start(0)
     backward(0, 3)
     backward(0, 1)
     gb.three()
+    ge[0].one()
     backward(1, 0)
+    gb.four()
+    e2_send(1)
+    xg_relay(0)
+    ge[0].two()
     backward(0, 2)
-    gb.four()
-    e2_send()
     backward(1, 3)
     backward(1, 1)
     backward(1, 2)
     make_d()
-    xg_relay(0)
     xg_start(1)
+    e2_start(1)
+    ge[0].three()
+    ge[0].four()
+    e2_share(0)
+    other_share()
     order = [(dy, dz) for dz in (2, 1, 3, 0) for dy in (1, 0)]
-    for n, (dy, dz) in enumerate(order[:4]):
+    for n, (dy, dz) in enumerate(order):
         ig_other(n, chip(dy, dz))
-    e2_start()
-    for n, (dy, dz) in enumerate(order[4:]):
-        ig_other(4 + n, chip(dy, dz))
-    other_share(1)
-    ge.one()
+
+    def ig_send(numbers):
+        for n in numbers:
+            dy, dz = order[n]
+            ig_own(n, chip(dy, dz))
+            if dz != 0:
+                igzc[(dy, dz)] = send(igr.at[chip(dy, dz)], igz.at[dz - 1, dy], dev(dz=dz))
+
+    ge[1].one()
+    wgrad(0, 0, first=True)
+    ig_send((0, 1))
+    ge[1].two()
+    ig_send((2, 3))
+    ge[1].three()
+    ge[1].four()
+    e2_share(1)
+    xg_rest(0)
+    xg_last(0)
+    other_wait(1)
+    wgrad(0, 1)
+    wgrad(0, 3)
+    wgrad(0, 2, last=True)
     xg_relay(1)
     xg_start(2)
-    for n, (dy, dz) in enumerate(order):
-        ig_own(n, chip(dy, dz))
-        if dz != 0:
-            igzc[(dy, dz)] = send(igr.at[chip(dy, dz)], igz.at[dz - 1, dy], dev(dz=dz))
-        if n == 3:
-            ge.two()
-    ge.three()
-    ge.four()
-    e2_share()
-    other_share(0)
-    other_wait(1)
-    wgrad(0, 0, first=True)
-    xg_rest(0)
-    wgrad(0, 1)
-    wgrad(0, 3)
-    xg_last(0)
-    e2_wait()
-    wgrad(0, 2, last=True)
+    ig_send((4, 5, 6, 7))
     other_wait(0)
     wgrad(1, 0, first=True)
     xg_rest(1)
     wgrad(1, 1)
     wgrad(1, 3)
+    xg_last(1)
+    wgrad(1, 2, last=True)
+    wgrad(2, 0, first=True)
     xg_relay(2)
     xg_start(3)
-    xg_last(1)
-    wgrad(1, 2, last=True)
     final(0)
+    load(upd_out_o, upd_out_h)
     ig_final_1()
-    wgrad(2, 0, first=True)
     xg_rest(2)
     wgrad(2, 1)
     wgrad(2, 3)
-    xg_relay(3)
     xg_last(2)
     wgrad(2, 2, last=True)
-    ig_final_2()
-    final(1)
     wgrad(3, 0, first=True)
+    xg_relay(3)
     xg_rest(3)
     wgrad(3, 1)
     wgrad(3, 3)
     xg_last(3)
     wgrad(3, 2, last=True)
+    ig_final_2()
+    load(ig_o, ig_h)
+    final(1)
+    load(upd_in_o.at[1], upd_in_h.at[1])
     final(2)
     final(3)
+    load(upd_in_o.at[0], upd_in_h.at[0])
 
     first = [
         send(rbuf.at[0], rbuf.at[1], dev(dc=1)),
@@ -553,13 +599,14 @@
     rmax_o[...] = jnp.maximum(jnp.maximum(rbuf[4], rbuf[5]), jnp.maximum(rbuf[6], rbuf[7]))
     cmax_o[...] = jnp.maximum(jnp.maximum(cbuf[2], cbuf[3]), jnp.maximum(cbuf[4], cbuf[5]))
 
-    for copy in sent:
+    for copy in loads[5:]:
+        copy.wait()
+    for copy in sent[-SENDING:]:
         copy.wait_send()
-    for t in range(2):
-        for taken, copy in xsent[t]:
-            @pl.when(taken)
-            def _(copy=copy):
-                copy.wait_send()
+    for taken, copy in xsent:
+        @pl.when(taken)
+        def _(copy=copy):
+            copy.wait_send()
 
 
 def finish(
@@ -602,7 +649,7 @@
         functools.partial(kernel, factor),
         out_shape=shapes,
         in_specs=[hbm] * 4 + [vmem] * 4,
-        out_specs=[vmem] * 5,
+        out_specs=[hbm] * 3 + [vmem] * 2,
         scratch_shapes=[
             pltpu.VMEM((2, 2, 8, t_rows, 256), BF),
             pltpu.VMEM(w_in.shape, BF),
@@ -621,11 +668,14 @@
             pltpu.VMEM((4, 512, 128), F32),
             pltpu.VMEM((8, 8, h_cols), F32),
             pltpu.VMEM((6, 8, h_cols), F32),
+        ]
+        + [pltpu.VMEM(s.shape, BF) for s in shapes[:3]]
+        + [
+            pltpu.SemaphoreType.DMA((9,)),
+            pltpu.SemaphoreType.DMA((SENDING,)),
+            pltpu.SemaphoreType.DMA((MESSAGES,)),
             pltpu.SemaphoreType.DMA((8,)),
-            pltpu.SemaphoreType.DMA((140,)),
-            pltpu.SemaphoreType.DMA((140,)),
-            pltpu.SemaphoreType.DMA((2, 8)),
-            pltpu.SemaphoreType.DMA((2, 2, 2)),
+            pltpu.SemaphoreType.DMA((2, 2)),
         ],
         compiler_params=pltpu.CompilerParams(
             collective_id=0, has_side_effects=True, vmem_limit_bytes=62 * 2**20

time: 165 us -> 153 us (0.927)
  Pallas kernels: 164 us -> 152 us
    pallas_call x1, Pallas kernels: 159 us -> 147 us  [local(): pl.pallas_call(functools.partial(kernel, factor), out_shape=shapes, in_sp...]
where the time goes in v3:
time: 153 us; the launch traced here: 152 us
  Pallas kernels  152 us (99%)
    pallas_call x1, Pallas kernels, local(): pl.pallas_call(functools.partial(kernel, factor), out_shape=shapes, in_sp...  147 us
    pallas_call x1, Pallas kernels, local(): pl.pallas_call(finish, out_shape=shapes[:3] + (jax.ShapeDtypeStruct(row_i...  4.07 us

profile of v3, /device:TPU:0, one launch (start us, length us, event | category | flops | bytes accessed | tf_op | source)
XLA Modules:
  0.0 152.3 jit_solution(17308723850255225803)
XLA Ops:
  0.6 147.4 %shard_map.135 = (bf16[512,256]{1,0:T(8,128)(2,1)}, bf16[2,512,640]{2,1,0:T(8,128)(2,1)}, bf16[640,512]{1,0:T(8,128)(2,1)}, f32[8,640]{1,0:T(8,128)}, f32[8,640]{1,0:T(8,128)}) custom-call(bf16[512,256]{1,0:T(8,128)(2,1)} %tok_in.1, bf16[512,256]{1,0:T(8,128)(2,1)} %cot_in.1, bf16[2,4096,640]{2,1,0:T(8,128)(2,1)} %w_in.1, bf16[640,4096]{1,0:T(8,128)(2,1)} %w_out.1, ...), custom_call_target="tpu_custom_call" | custom-call | flops 21500000256 | bytes 22000000 | tf_op jit(solution)/shard_map/pallas_call | solution.py:648
  148.1 4.1 %shard_map.136 = (bf16[512,256]{1,0:T(8,128)(2,1)}, bf16[2,512,640]{2,1,0:T(8,128)(2,1)}, bf16[640,512]{1,0:T(8,128)(2,1)}, f32[2,512]{1,0:T(2,128)}, f32[2,640]{1,0:T(2,128)}, /*index=5*/f32[640]{0:T(1024)}, f32[512]{0:T(512)}) custom-call(bf16[512,256]{1,0:T(8,128)(2,1)} %get-tuple-element.12.ig, bf16[2,512,640]{2,1,0:T(8,128)(2,1)} %get-tuple-element.13.upd_in, ...), custom_call_target="tpu_custom_call" | custom-call | tf_op jit(solution)/shard_map/pallas_call | solution.py:687

commit v4 on v3

--- a/solution.py
+++ b/solution.py
@@ -50,7 +50,9 @@
     wi,
     wo,
     pre,
+    own,
     act,
+    kept,
     other,
     accs,
     gsend,
@@ -59,8 +61,7 @@
     igr,
     igz,
     igy,
-    rowv,
-    rowm,
+    colv,
     rbuf,
     cbuf,
     ig_o,
@@ -288,38 +289,48 @@
             else:
                 pre[2, rows] += part
 
-    step = 32
+    def blocks(body):
+        n = h_cols // 128
+
+        @pl.loop(0, (t_rows // 128) * n)
+        def _(i):
+            body(
+                pl.ds(pl.multiple_of(i // n * 128, 128), 128),
+                pl.ds(pl.multiple_of(lax.rem(i, n) * 128, 128), 128),
+            )
 
     def make_hidden():
-        @pl.loop(0, t_rows // step)
-        def _(i):
-            rows = pl.ds(pl.multiple_of(i * step, step), step)
-            v = pre[0, rows]
-            up = pre[1, rows]
+        def body(rows, cols):
+            v = pre[0, rows, cols]
+            up = pre[1, rows, cols]
             t = jnp.tanh(ROOT * (v + 0.044715 * v * v * v))
             activated = 0.5 * v * (1.0 + t)
             slopes = 0.5 * (1.0 + t) + 0.5 * v * (1.0 - t * t) * ROOT * (
                 1.0 + 3.0 * 0.044715 * v * v
             )
-            act[HID, 0, rows] = (activated * up).astype(BF)
-            pre[0, rows] = activated
-            pre[1, rows] = up * slopes
+            act[HID, 0, cols, rows] = (activated * up).T.astype(BF)
+            pre[0, rows, cols] = activated
+            pre[1, rows, cols] = up * slopes
+
+        blocks(body)
 
     def make_d():
-        @pl.loop(0, t_rows // step)
-        def _(i):
-            rows = pl.ds(pl.multiple_of(i * step, step), step)
-            d = pre[2, rows]
-            act[DUP, 0, rows] = (d * pre[0, rows]).astype(BF)
-            act[DGATE, 0, rows] = (d * pre[1, rows]).astype(BF)
+        def body(rows, cols):
+            d = pre[2, rows, cols]
+            for i in range(2):
+                value = d * pre[i, rows, cols]
+                own[i, rows, cols] = value.astype(BF)
+                act[DUP + i, 0, cols, rows] = value.T.astype(BF)
+
+        blocks(body)
 
     xg = [{} for _ in PIECES]
-    lo, hi = pl.ds(0, half), pl.ds(half, half)
-
-    def xg_send(p, name, source, there, rows, device):
-        q, first_col, cols = PIECES[p]
-        cut = pl.ds(first_col, cols)
-        xg[p][name] = send(act.at[q, source, rows, cut], act.at[q, there, rows, cut], device)
+    lo, hi = 0, 1
+
+    def xg_send(p, name, source, there, part, device):
+        q, first_unit, units = PIECES[p]
+        cut = pl.ds(first_unit + part * (units // 2), units // 2)
+        xg[p][name] = send(act.at[q, source, cut], act.at[q, there, cut], device)
 
     def xg_start(p):
         xg_send(p, "a-", 0, 1, lo, dev(dx=1))
@@ -363,35 +374,35 @@
     gs = [None] * len(PIECES)
 
     def wgrad(p, r, first=False, last=False):
-        q, first_col, n = PIECES[p]
-        cut = pl.ds(first_col, n)
+        q, first_unit, n = PIECES[p]
+        cut = pl.ds(first_unit, n)
         t = 1 if q == HID else 0
 
         @pl.loop(0, 4)
         def _(i):
             part_kept, b = i // 2, i % 2
             h = jnp.where(part_kept == 1, yh, 1 - yh)
-            rows = pl.ds(pl.multiple_of(b * 256, 256), 256)
+            cols = pl.ds(pl.multiple_of(b * 256, 256), 256)
             if r == 0:
-                left = full[t, h, 2 * x + b]
+                right = full[t, h, 2 * x + b]
             else:
-                left = other[t, r - 1, h, b]
-            part = tn(left, act[q, r, :, cut]) * factor
+                right = other[t, r - 1, h, b]
+            part = nn(act[q, r, cut], right) * factor
 
             @pl.when(part_kept == 1)
             def _():
-                pre[q, rows, cut] = part if first else pre[q, rows, cut] + part
+                kept[q, cut, cols] = part if first else kept[q, cut, cols] + part
 
             @pl.when(part_kept == 0)
             def _():
-                total = part if first else accs[rows, cut] + part
+                total = part if first else accs[cut, cols] + part
                 if last:
-                    gsend[q, rows, cut] = total.astype(BF)
+                    gsend[q, cut, cols] = total.astype(BF)
                 else:
-                    accs[rows, cut] = total
+                    accs[cut, cols] = total
 
         if last:
-            gs[p] = send(gsend.at[q, :, cut], grecv.at[q, :, cut], dev(dyh=1))
+            gs[p] = send(gsend.at[q, cut], grecv.at[q, cut], dev(dyh=1))
 
     def shard_rows(shard):
         return pl.ds(pl.multiple_of(shard * 256, 256), 256)
@@ -401,7 +412,7 @@
     def ig_other(n, m):
         shard = 2 * m + 1 - c
         igs[m] = (
-            nt(act[DGATE, 0], wi[0, shard_rows(shard)]) + nt(act[DUP, 0], wi[1, shard_rows(shard)])
+            nt(own[1], wi[0, shard_rows(shard)]) + nt(own[0], wi[1, shard_rows(shard)])
         ).astype(BF)
         igc[n] = send(igs.at[m], igr.at[m], dev(dc=1))
 
@@ -410,7 +421,7 @@
     def ig_own(n, m):
         igc[n].wait_recv()
         shard = 2 * m + c
-        total = nt(act[DGATE, 0], wi[0, shard_rows(shard)]) + nt(act[DUP, 0], wi[1, shard_rows(shard)])
+        total = nt(own[1], wi[0, shard_rows(shard)]) + nt(own[0], wi[1, shard_rows(shard)])
         igr[m] = (total + igr[m].astype(F32)).astype(BF)
 
     def ig_final_1():
@@ -425,45 +436,37 @@
                 igy[0] = total.astype(BF)
                 igzc["y"] = send(igy.at[0], igy.at[1], dev(dyl=1))
             else:
-                rowm[2], rowm[3] = total[:, :128], total[:, 128:]
+                pre[0, :, pl.ds(0, 256)] = total
 
     def ig_final_2():
         igzc["y"].wait_recv()
-        for i in range(2):
-            cols = pl.ds(i * 128, 128)
-            ig_o[:, cols] = (rowm[2 + i] + igy[1, :, cols].astype(F32)).astype(BF)
-
-    fin = 64
+        ig_o[...] = (pre[0, :, pl.ds(0, 256)] + igy[1].astype(F32)).astype(BF)
+
+    fin = 128
 
     def final(p):
-        q, first_col, n = PIECES[p]
-        cut = pl.ds(first_col, n)
+        q, first_unit, n = PIECES[p]
         gs[p].wait_recv()
-        col = row_out[...].reshape(1, h_cols) if q == HID else col_in[pl.ds(2 - q, 1), cut]
-
-        def body(i, colmax):
-            rows = pl.ds(pl.multiple_of(i * fin, fin), fin)
-            g = pre[q, rows, cut] + grecv[q, rows, cut].astype(F32)
-            nu = jnp.minimum(rowv[q, rows][:, :1], col) + g * g
+        row = col_out[...].reshape(1, 512) if q == HID else row_in[pl.ds(2 - q, 1)]
+
+        def body(i, rowmax):
+            units = pl.ds(pl.multiple_of(first_unit + i * fin, fin), fin)
+            g = kept[q, units] + grecv[q, units].astype(F32)
+            nu = jnp.minimum(colv[q, units][:, :1], row) + g * g
             upd = g * lax.rsqrt(nu)
             if q == HID:
-                pre[q, rows] = upd
+                upd_out_o[units] = upd.astype(BF)
             else:
-                upd_in_o[2 - q, rows, cut] = upd.astype(BF)
-            rowm[p, rows] = jnp.broadcast_to(jnp.max(nu, axis=1, keepdims=True), (fin, 128))
-            return jnp.maximum(colmax, jnp.max(nu, axis=0, keepdims=True))
-
-        colmax = lax.fori_loop(0, 512 // fin, body, jnp.zeros((1, n), F32))
-        cbuf[0, pl.ds(q, 1), cut] = colmax
-        rowmax = rowm[p].T[:1]
-        if first_col != 0:
+                upd_in_o[2 - q, :, units] = upd.T.astype(BF)
+            colv[q, units] = jnp.broadcast_to(jnp.max(nu, axis=1, keepdims=True), (fin, 128))
+            return jnp.maximum(rowmax, jnp.max(nu, axis=0, keepdims=True))
+
+        rowmax = lax.fori_loop(0, n // fin, body, jnp.zeros((1, 512), F32))
+        cut = pl.ds(first_unit, n)
+        cbuf[0, pl.ds(q, 1), cut] = colv[q, cut].T[:1]
+        if first_unit != 0:
             rowmax = jnp.maximum(rowmax, rbuf[0, pl.ds(q, 1), pl.ds(0, 512)])
         rbuf[0, pl.ds(q, 1), pl.ds(0, 512)] = rowmax
-        if q == HID:
-            @pl.loop(0, h_cols // 128)
-            def _(j):
-                cols = pl.ds(pl.multiple_of(j * 128, 128), 128)
-                upd_out_o[cols] = pre[q, :, cols].T.astype(BF)
 
     pl.semaphore_wait(barrier, len(peers))
     ga.start(tok_in)
@@ -471,8 +474,8 @@
     cbuf[0] = jnp.zeros_like(cbuf[0])
     rbuf[0] = jnp.zeros_like(rbuf[0])
     for q in range(3):
-        row = col_out[...].reshape(1, 512) if q == HID else row_in[pl.ds(2 - q, 1)]
-        rowv[q] = jnp.broadcast_to(row, (128, 512)).T
+        col = row_out[...].reshape(1, h_cols) if q == HID else col_in[pl.ds(2 - q, 1)]
+        colv[q] = jnp.broadcast_to(col, (128, h_cols)).T
     own_tok.wait()
     own_cot.wait()
     ga.one()
@@ -655,17 +658,18 @@
             pltpu.VMEM(w_in.shape, BF),
             pltpu.VMEM(w_out.shape, BF),
             pltpu.VMEM((3, t_rows, h_cols), F32),
-            pltpu.VMEM((3, 4, t_rows, h_cols), BF),
+            pltpu.VMEM((2, t_rows, h_cols), BF),
+            pltpu.VMEM((3, 4, h_cols, t_rows), BF),
+            pltpu.VMEM((3, h_cols, 512), F32),
             pltpu.VMEM((2, 3, 2, 2, t_rows, 256), BF),
-            pltpu.VMEM((512, h_cols), F32),
-            pltpu.VMEM((3, 512, h_cols), BF),
-            pltpu.VMEM((3, 512, h_cols), BF),
+            pltpu.VMEM((h_cols, 512), F32),
+            pltpu.VMEM((3, h_cols, 512), BF),
+            pltpu.VMEM((3, h_cols, 512), BF),
             pltpu.VMEM((8, t_rows, 256), BF),
             pltpu.VMEM((8, t_rows, 256), BF),
             pltpu.VMEM((3, 2, t_rows, 256), BF),
             pltpu.VMEM((2, t_rows, 256), BF),
-            pltpu.VMEM((3, 512, 128), F32),
-            pltpu.VMEM((4, 512, 128), F32),
+            pltpu.VMEM((3, h_cols, 128), F32),
             pltpu.VMEM((8, 8, h_cols), F32),
             pltpu.VMEM((6, 8, h_cols), F32),
         ]

time: 153 us -> 156 us (1.020)
  Pallas kernels: 152 us -> 154 us
    pallas_call x1, Pallas kernels: 147 us -> 150 us  [local(): pl.pallas_call(functools.partial(kernel, factor), out_shape=shapes, in_sp...]
where the time goes in v4:
time: 156 us; the launch traced here: 154 us
  Pallas kernels  154 us (99%)
    pallas_call x1, Pallas kernels, local(): pl.pallas_call(functools.partial(kernel, factor), out_shape=shapes, in_sp...  150 us
    pallas_call x1, Pallas kernels, local(): pl.pallas_call(finish, out_shape=shapes[:3] + (jax.ShapeDtypeStruct(row_i...  4.07 us

profile of v4, /device:TPU:0, one launch (start us, length us, event | category | flops | bytes accessed | tf_op | source)
XLA Modules:
  0.0 154.5 jit_solution(8037072193436550080)
XLA Ops:
  0.6 149.6 %shard_map.135 = (bf16[512,256]{1,0:T(8,128)(2,1)}, bf16[2,512,640]{2,1,0:T(8,128)(2,1)}, bf16[640,512]{1,0:T(8,128)(2,1)}, f32[8,640]{1,0:T(8,128)}, f32[8,640]{1,0:T(8,128)}) custom-call(bf16[512,256]{1,0:T(8,128)(2,1)} %tok_in.1, bf16[512,256]{1,0:T(8,128)(2,1)} %cot_in.1, bf16[2,4096,640]{2,1,0:T(8,128)(2,1)} %w_in.1, bf16[640,4096]{1,0:T(8,128)(2,1)} %w_out.1, ...), custom_call_target="tpu_custom_call" | custom-call | flops 21500000256 | bytes 22000000 | tf_op jit(solution)/shard_map/pallas_call | solution.py:651
  150.2 4.1 %shard_map.136 = (bf16[512,256]{1,0:T(8,128)(2,1)}, bf16[2,512,640]{2,1,0:T(8,128)(2,1)}, bf16[640,512]{1,0:T(8,128)(2,1)}, f32[2,512]{1,0:T(2,128)}, f32[2,640]{1,0:T(2,128)}, /*index=5*/f32[640]{0:T(1024)}, f32[512]{0:T(512)}) custom-call(bf16[512,256]{1,0:T(8,128)(2,1)} %get-tuple-element.12.ig, bf16[2,512,640]{2,1,0:T(8,128)(2,1)} %get-tuple-element.13.upd_in, ...), custom_call_target="tpu_custom_call" | custom-call | tf_op jit(solution)/shard_map/pallas_call | solution.py:691

commit v5 on v3

--- a/solution.py
+++ b/solution.py
@@ -362,7 +362,7 @@
 
     gs = [None] * len(PIECES)
 
-    def wgrad(p, r, first=False, last=False):
+    def wgrad(p, *sources, first=False, last=False):
         q, first_col, n = PIECES[p]
         cut = pl.ds(first_col, n)
         t = 1 if q == HID else 0
@@ -372,11 +372,11 @@
             part_kept, b = i // 2, i % 2
             h = jnp.where(part_kept == 1, yh, 1 - yh)
             rows = pl.ds(pl.multiple_of(b * 256, 256), 256)
-            if r == 0:
-                left = full[t, h, 2 * x + b]
-            else:
-                left = other[t, r - 1, h, b]
-            part = tn(left, act[q, r, :, cut]) * factor
+            part = None
+            for r in sources:
+                left = full[t, h, 2 * x + b] if r == 0 else other[t, r - 1, h, b]
+                term = tn(left, act[q, r, :, cut])
+                part = term if part is None else part + term
 
             @pl.when(part_kept == 1)
             def _():
@@ -386,7 +386,7 @@
             def _():
                 total = part if first else accs[rows, cut] + part
                 if last:
-                    gsend[q, rows, cut] = total.astype(BF)
+                    gsend[q, rows, cut] = (total * factor).astype(BF)
                 else:
                     accs[rows, cut] = total
 
@@ -443,7 +443,7 @@
 
         def body(i, colmax):
             rows = pl.ds(pl.multiple_of(i * fin, fin), fin)
-            g = pre[q, rows, cut] + grecv[q, rows, cut].astype(F32)
+            g = pre[q, rows, cut] * factor + grecv[q, rows, cut].astype(F32)
             nu = jnp.minimum(rowv[q, rows][:, :1], col) + g * g
             upd = g * lax.rsqrt(nu)
             if q == HID:
@@ -510,18 +510,16 @@
     ge[0].two()
     backward(0, 2)
     backward(1, 3)
+    e2_start(1)
     backward(1, 1)
     backward(1, 2)
     make_d()
     xg_start(1)
-    e2_start(1)
-    ge[0].three()
-    ge[0].four()
-    e2_share(0)
-    other_share()
     order = [(dy, dz) for dz in (2, 1, 3, 0) for dy in (1, 0)]
     for n, (dy, dz) in enumerate(order):
         ig_other(n, chip(dy, dz))
+        if n == 3:
+            ge[1].one()
 
     def ig_send(numbers):
         for n in numbers:
@@ -530,28 +528,27 @@
             if dz != 0:
                 igzc[(dy, dz)] = send(igr.at[chip(dy, dz)], igz.at[dz - 1, dy], dev(dz=dz))
 
-    ge[1].one()
+    ge[1].two()
     wgrad(0, 0, first=True)
+    ge[0].three()
+    ge[0].four()
+    e2_share(0)
+    other_share()
     ig_send((0, 1))
-    ge[1].two()
-    ig_send((2, 3))
     ge[1].three()
     ge[1].four()
     e2_share(1)
     xg_rest(0)
     xg_last(0)
-    other_wait(1)
-    wgrad(0, 1)
-    wgrad(0, 3)
-    wgrad(0, 2, last=True)
     xg_relay(1)
     xg_start(2)
-    ig_send((4, 5, 6, 7))
+    other_wait(1)
+    wgrad(0, 1, 2, 3, last=True)
+    ig_send((2, 3, 4, 5, 6, 7))
     other_wait(0)
     wgrad(1, 0, first=True)
     xg_rest(1)
-    wgrad(1, 1)
-    wgrad(1, 3)
+    wgrad(1, 1, 3)
     xg_last(1)
     wgrad(1, 2, last=True)
     wgrad(2, 0, first=True)
@@ -559,17 +556,15 @@
     xg_start(3)
     final(0)
     load(upd_out_o, upd_out_h)
-    ig_final_1()
     xg_rest(2)
-    wgrad(2, 1)
-    wgrad(2, 3)
+    wgrad(2, 1, 3)
     xg_last(2)
     wgrad(2, 2, last=True)
     wgrad(3, 0, first=True)
     xg_relay(3)
+    ig_final_1()
     xg_rest(3)
-    wgrad(3, 1)
-    wgrad(3, 3)
+    wgrad(3, 1, 3)
     xg_last(3)
     wgrad(3, 2, last=True)
     ig_final_2()

time: 153 us -> 149 us (0.974)
  Pallas kernels: 152 us -> 147 us
    pallas_call x1, Pallas kernels: 147 us -> 143 us  [local(): pl.pallas_call(functools.partial(kernel, factor), out_shape=shapes, in_sp...]
where the time goes in v5:
time: 149 us; the launch traced here: 148 us
  Pallas kernels  147 us (99%)
    pallas_call x1, Pallas kernels, local(): pl.pallas_call(functools.partial(kernel, factor), out_shape=shapes, in_sp...  143 us
    pallas_call x1, Pallas kernels, local(): pl.pallas_call(finish, out_shape=shapes[:3] + (jax.ShapeDtypeStruct(row_i...  4.07 us

profile of v5, /device:TPU:0, one launch (start us, length us, event | category | flops | bytes accessed | tf_op | source)
XLA Modules:
  0.0 148.1 jit_solution(847553605060301412)
XLA Ops:
  0.6 143.2 %shard_map.135 = (bf16[512,256]{1,0:T(8,128)(2,1)}, bf16[2,512,640]{2,1,0:T(8,128)(2,1)}, bf16[640,512]{1,0:T(8,128)(2,1)}, f32[8,640]{1,0:T(8,128)}, f32[8,640]{1,0:T(8,128)}) custom-call(bf16[512,256]{1,0:T(8,128)(2,1)} %tok_in.1, bf16[512,256]{1,0:T(8,128)(2,1)} %cot_in.1, bf16[2,4096,640]{2,1,0:T(8,128)(2,1)} %w_in.1, bf16[640,4096]{1,0:T(8,128)(2,1)} %w_out.1, ...), custom_call_target="tpu_custom_call" | custom-call | flops 21500000256 | bytes 22000000 | tf_op jit(solution)/shard_map/pallas_call | solution.py:643
  143.9 4.1 %shard_map.136 = (bf16[512,256]{1,0:T(8,128)(2,1)}, bf16[2,512,640]{2,1,0:T(8,128)(2,1)}, bf16[640,512]{1,0:T(8,128)(2,1)}, f32[2,512]{1,0:T(2,128)}, f32[2,640]{1,0:T(2,128)}, /*index=5*/f32[640]{0:T(1024)}, f32[512]{0:T(512)}) custom-call(bf16[512,256]{1,0:T(8,128)(2,1)} %get-tuple-element.12.ig, bf16[2,512,640]{2,1,0:T(8,128)(2,1)} %get-tuple-element.13.upd_in, ...), custom_call_target="tpu_custom_call" | custom-call | tf_op jit(solution)/shard_map/pallas_call | solution.py:682

commit v6 on v5

--- a/solution.py
+++ b/solution.py
@@ -37,10 +37,10 @@
     cot_in,
     w_in,
     w_out,
-    row_in,
-    col_in,
-    row_out,
-    col_out,
+    row_in_h,
+    col_in_h,
+    row_out_h,
+    col_out_h,
     ig_h,
     upd_in_h,
     upd_out_h,
@@ -66,6 +66,10 @@
     ig_o,
     upd_in_o,
     upd_out_o,
+    row_in,
+    col_in,
+    row_out,
+    col_out,
     lsem,
     ssem,
     rsem,
@@ -105,6 +109,10 @@
 
     own_tok = load(tok_in, full.at[0, yl, z * 2 + c])
     own_cot = load(cot_in, full.at[1, yl, z * 2 + c])
+    load_small = [
+        load(row_in_h, row_in), load(col_in_h, col_in),
+        load(row_out_h, row_out), load(col_out_h, col_out),
+    ]
 
     sent = []
 
@@ -470,6 +478,8 @@
     load_w = [load(w_in.at[0], wi.at[0]), load(w_in.at[1], wi.at[1])]
     cbuf[0] = jnp.zeros_like(cbuf[0])
     rbuf[0] = jnp.zeros_like(rbuf[0])
+    for copy in load_small:
+        copy.wait()
     for q in range(3):
         row = col_out[...].reshape(1, 512) if q == HID else row_in[pl.ds(2 - q, 1)]
         rowv[q] = jnp.broadcast_to(row, (128, 512)).T
@@ -520,6 +530,8 @@
         ig_other(n, chip(dy, dz))
         if n == 3:
             ge[1].one()
+            wgrad(0, 0, first=True)
+            ge[1].two()
 
     def ig_send(numbers):
         for n in numbers:
@@ -528,13 +540,10 @@
             if dz != 0:
                 igzc[(dy, dz)] = send(igr.at[chip(dy, dz)], igz.at[dz - 1, dy], dev(dz=dz))
 
-    ge[1].two()
-    wgrad(0, 0, first=True)
     ge[0].three()
     ge[0].four()
     e2_share(0)
     other_share()
-    ig_send((0, 1))
     ge[1].three()
     ge[1].four()
     e2_share(1)
@@ -544,7 +553,7 @@
     xg_start(2)
     other_wait(1)
     wgrad(0, 1, 2, 3, last=True)
-    ig_send((2, 3, 4, 5, 6, 7))
+    ig_send(range(8))
     other_wait(0)
     wgrad(1, 0, first=True)
     xg_rest(1)
@@ -594,7 +603,7 @@
     rmax_o[...] = jnp.maximum(jnp.maximum(rbuf[4], rbuf[5]), jnp.maximum(rbuf[6], rbuf[7]))
     cmax_o[...] = jnp.maximum(jnp.maximum(cbuf[2], cbuf[3]), jnp.maximum(cbuf[4], cbuf[5]))
 
-    for copy in loads[5:]:
+    for copy in loads[9:]:
         copy.wait()
     for copy in sent[-SENDING:]:
         copy.wait_send()
@@ -607,23 +616,30 @@
 def finish(
     ig, upd_in, upd_out, rmax, cmax,
     ig_o, upd_in_o, upd_out_o, row_in_o, col_in_o, row_out_o, col_out_o,
-    ig_v, upd_in_v, upd_out_v, sem,
+    ig_v, upd_in_v, upd_out_v, rmax_v, cmax_v, row_in_v, col_in_v, row_out_v, col_out_v, sem,
 ):
-    steps = ((ig, ig_v, ig_o), (upd_in, upd_in_v, upd_in_o), (upd_out, upd_out_v, upd_out_o))
-    ins = [pltpu.make_async_copy(s, v, sem.at[0, i]) for i, (s, v, o) in enumerate(steps)]
-    copies = [pltpu.make_async_copy(v, o, sem.at[1, i]) for i, (s, v, o) in enumerate(steps)]
+    ins = ((rmax, rmax_v), (cmax, cmax_v), (ig, ig_v), (upd_out, upd_out_v), (upd_in, upd_in_v))
+    ins = [pltpu.make_async_copy(s, d, sem.at[i]) for i, (s, d) in enumerate(ins)]
     for copy in ins:
         copy.start()
+    big = ((ig_v, ig_o), (upd_out_v, upd_out_o), (upd_in_v, upd_in_o))
+    small = (
+        (row_in_v, row_in_o), (col_in_v, col_in_o), (row_out_v, row_out_o), (col_out_v, col_out_o)
+    )
+    outs = [pltpu.make_async_copy(s, d, sem.at[5 + i]) for i, (s, d) in enumerate(small + big)]
+    ins[0].wait()
+    ins[1].wait()
     n = row_in_o.shape[1]
-    col_out_o[...] = rmax[HID, pl.ds(0, n)]
-    row_out_o[...] = cmax[HID]
+    col_out_v[...] = rmax_v[HID, pl.ds(0, n)]
+    row_out_v[...] = cmax_v[HID]
     for q in (DUP, DGATE):
-        row_in_o[pl.ds(2 - q, 1)] = rmax[q : q + 1, :n]
-        col_in_o[pl.ds(2 - q, 1)] = cmax[q : q + 1]
-    for before, copy in zip(ins, copies):
-        before.wait()
+        row_in_v[pl.ds(2 - q, 1)] = rmax_v[q : q + 1, :n]
+        col_in_v[pl.ds(2 - q, 1)] = cmax_v[q : q + 1]
+    for i, copy in enumerate(outs):
+        if i >= 4:
+            ins[i - 2].wait()
         copy.start()
-    for copy in copies:
+    for copy in outs:
         copy.wait()
 
 
@@ -643,7 +659,7 @@
     out = pl.pallas_call(
         functools.partial(kernel, factor),
         out_shape=shapes,
-        in_specs=[hbm] * 4 + [vmem] * 4,
+        in_specs=[hbm] * 8,
         out_specs=[hbm] * 3 + [vmem] * 2,
         scratch_shapes=[
             pltpu.VMEM((2, 2, 8, t_rows, 256), BF),
@@ -665,8 +681,9 @@
             pltpu.VMEM((6, 8, h_cols), F32),
         ]
         + [pltpu.VMEM(s.shape, BF) for s in shapes[:3]]
+        + [pltpu.VMEM(a.shape, F32) for a in (row_in, col_in, row_out, col_out)]
         + [
-            pltpu.SemaphoreType.DMA((9,)),
+            pltpu.SemaphoreType.DMA((13,)),
             pltpu.SemaphoreType.DMA((SENDING,)),
             pltpu.SemaphoreType.DMA((MESSAGES,)),
             pltpu.SemaphoreType.DMA((8,)),
@@ -688,10 +705,12 @@
             jax.ShapeDtypeStruct(row_out.shape, F32),
             jax.ShapeDtypeStruct(col_out.shape, F32),
         ),
-        in_specs=[hbm] * 3 + [vmem] * 2,
-        out_specs=[hbm] * 3 + [vmem] * 4,
+        in_specs=[hbm] * 5,
+        out_specs=[hbm] * 7,
         scratch_shapes=[pltpu.VMEM(s.shape, BF) for s in shapes[:3]]
-        + [pltpu.SemaphoreType.DMA((2, 3))],
+        + [pltpu.VMEM(s.shape, F32) for s in shapes[3:]]
+        + [pltpu.VMEM(a.shape, F32) for a in (row_in, col_in, row_out, col_out)]
+        + [pltpu.SemaphoreType.DMA((12,))],
     )(*out)
 
 

time: 149 us -> 139 us (0.933)
  Pallas kernels: 147 us -> 138 us
    pallas_call x1, Pallas kernels: 143 us -> 135 us  [local(): pl.pallas_call(functools.partial(kernel, factor), out_shape=shapes, in_sp...]
where the time goes in v6:
time: 139 us
  Pallas kernels  138 us (99%)
    pallas_call x1, Pallas kernels, local(): pl.pallas_call(functools.partial(kernel, factor), out_shape=shapes, in_sp...  135 us
    pallas_call x1, Pallas kernels, local(): pl.pallas_call(finish, out_shape=shapes[:3] + (jax.ShapeDtypeStruct(row_i...  2.8 us

profile of v6, /device:TPU:0, one launch (start us, length us, event | category | flops | bytes accessed | tf_op | source)
XLA Modules:
  0.0 139.0 jit_solution(17984773593732708647)
XLA Ops:
  0.6 135.4 %shard_map.135 = (bf16[512,256]{1,0:T(8,128)(2,1)}, bf16[2,512,640]{2,1,0:T(8,128)(2,1)}, bf16[640,512]{1,0:T(8,128)(2,1)}, f32[8,640]{1,0:T(8,128)}, f32[8,640]{1,0:T(8,128)}) custom-call(bf16[512,256]{1,0:T(8,128)(2,1)} %tok_in.1, bf16[512,256]{1,0:T(8,128)(2,1)} %cot_in.1, bf16[2,4096,640]{2,1,0:T(8,128)(2,1)} %w_in.1, bf16[640,4096]{1,0:T(8,128)(2,1)} %w_out.1, ...), custom_call_target="tpu_custom_call" | custom-call | flops 21500000256 | bytes 22000000 | tf_op jit(solution)/shard_map/pallas_call | solution.py:659
  136.1 2.8 %shard_map.136 = (bf16[512,256]{1,0:T(8,128)(2,1)}, bf16[2,512,640]{2,1,0:T(8,128)(2,1)}, bf16[640,512]{1,0:T(8,128)(2,1)}, f32[2,512]{1,0:T(2,128)}, f32[2,640]{1,0:T(2,128)}, /*index=5*/f32[640]{0:T(1024)}, f32[512]{0:T(512)}) custom-call(bf16[512,256]{1,0:T(8,128)(2,1)} %get-tuple-element.12.ig, bf16[2,512,640]{2,1,0:T(8,128)(2,1)} %get-tuple-element.13.upd_in, ...), custom_call_target="tpu_custom_call" | custom-call | tf_op jit(solution)/shard_map/pallas_call | solution.py:699
